TPU v7x, 256 devices: a whole 4x4x8 slice. The times are simulated.
256 devices in a mesh: dom: 64 (over z, x, core), grp: 4 (over y).
Axes of the slice: x: 4, y: 4, z: 8, core: 2. Of those that a mesh axis runs over, the one named last changes fastest.
Arguments:
- features: bfloat16 [262144, 512], P(('dom', 'grp')), may hold values from -6 to 6
- tile_src: int32 [2048, 8], P(('dom', 'grp')), may hold values from 0 to 15
- tile_val: bfloat16 [2048, 8, 128, 128], P(('dom', 'grp')), may hold values from -0.1875 to 0.1875
- send_sel: int32 [256, 64], P(('dom', 'grp')), may hold values from 0 to 63
- stale_features: bfloat16 [262144, 512], P(('dom', 'grp')), may hold values from -5 to 5
- stale_grads: bfloat16 [262144, 512], P(('dom', 'grp')), may hold values from -6 to 6
- out_grad: bfloat16 [262144, 512], P(('dom', 'grp')), may hold values from -6 to 6
- master: float32 [2, 512, 512], P(None, ('dom', 'grp')), may hold values from -0.25 to 0.25
- moment_first: float32 [2, 512, 512], P(None, ('dom', 'grp')), may hold values from -0.0078125 to 0.0078125
- moment_second: float32 [2, 512, 512], P(None, ('dom', 'grp')), may hold values from 7.6293944e-08 to 1.9073486e-06
Outputs:
- layer_out: bfloat16 [262144, 512], P(('dom', 'grp'))
- fresh_features: bfloat16 [262144, 512], P(('dom', 'grp'))
- fresh_grads: bfloat16 [262144, 512], P(('dom', 'grp'))
- master_next: float32 [2, 512, 512], P(None, ('dom', 'grp'))
- weights_next: bfloat16 [2, 512, 512], replicated
Inputs may be any that keep to these rules, and one draw needn't show every extreme that they name: `tile_src`: A value below 8 names a local row block; 8 + b names boundary block b.
All inputs are finite; a program needn't handle non-finite values.
Results may differ from a plain program's by a relative error of at most 0.005.
The roundings to bfloat16 on the way count: a program that leaves them out, or rounds other values in their place, can miss the bound.
Values may be sent and summed in bfloat16 or wider, within the bound.
A program may use at most 128 MiB of HBM per device.

v0:
```python
import jax
import jax.numpy as jnp
from jax import lax
from jax.sharding import Mesh
from jax.sharding import PartitionSpec as P

STEP = 10
DOM = ("dom_0", "dom_1", "dom_2")
DOM_GRP = ("dom_0", "dom_1", "dom_2", "grp")


decay_first = 0.9
decay_second = 0.95
learn_rate = 0.01
epsilon = 1e-08


def from_everyone(array, axis):
    peers = lax.axis_size(axis)
    return lax.all_to_all(
        jnp.broadcast_to(array[None], (peers, *array.shape)), axis, 0, 0, tiled=True
    )


def joined_along(tiles, dim):
    lengths = list(tiles.shape[1:])
    lengths[dim] *= tiles.shape[0]
    return jnp.moveaxis(tiles, 0, dim).reshape(lengths)


def whole_of(array, axes, dim):
    far, near = axes
    leading = from_everyone(array, far)
    tiles = jnp.swapaxes(from_everyone(leading, near), 0, 1)
    return joined_along(tiles.reshape(-1, *array.shape), dim)


def in_blocks(array, dim, peers):
    lengths = array.shape
    tiles = array.reshape(*lengths[:dim], peers, lengths[dim] // peers, *lengths[dim + 1 :])
    return jnp.moveaxis(tiles, dim, 0)


def sent_and_summed(array, axis, dim):
    tiles = in_blocks(array, dim, lax.axis_size(axis))
    arrived = lax.all_to_all(tiles, axis, split_axis=0, concat_axis=0, tiled=True)
    return arrived.astype(jnp.float32).sum(axis=0)


def summed_rows(array, axes, dim):
    far, near = axes
    tiles = in_blocks(array, dim, lax.axis_size(far))
    nearer = sent_and_summed(tiles, near, dim + 1)
    arrived = lax.all_to_all(
        nearer.astype(jnp.bfloat16), far, split_axis=0, concat_axis=0, tiled=True
    )
    return arrived.astype(jnp.float32).sum(axis=0)


def aggregate(local_rows, rim_rows, tile_val, tile_src):
    edge = tile_val.shape[2]
    lookup = jnp.concatenate([local_rows, rim_rows], 0).reshape(-1, edge, local_rows.shape[1])
    picked = lookup[tile_src]
    total = jnp.einsum("rtij,rtjf->rif", tile_val, picked, preferred_element_type=jnp.float32)
    return total.reshape(-1, local_rows.shape[1])


def per_device(
    features,
    tile_src,
    tile_val,
    send_sel,
    stale_features,
    stale_grads,
    out_grad,
    master,
    moment_first,
    moment_second,
):
    peers = lax.axis_size(DOM)
    devices = peers * lax.axis_size("grp")
    total_nodes = features.shape[0] * devices
    feature_width = features.shape[1]
    blocks, tiles_row, edge = (tile_val.shape[0], tile_val.shape[1], tile_val.shape[2])
    piece_rows = stale_features.shape[0] // peers
    local_count = features.shape[0]
    selects = send_sel[0]
    weights = whole_of(master.astype(jnp.bfloat16), (("dom_0", "dom_1"), ("dom_2", "grp")), 1)
    w_first, w_second = (weights[0], weights[1])

    def outgoing(node_rows):
        pieces = node_rows.reshape(-1, piece_rows, feature_width)
        return jnp.take(pieces, selects, axis=0)

    raw_rim = lax.all_to_all(
        outgoing(features), DOM, split_axis=0, concat_axis=0, tiled=True
    ).reshape(-1, feature_width)
    p_first = aggregate(features, raw_rim, tile_val, tile_src).astype(jnp.bfloat16)
    z_first = jnp.dot(p_first, w_first, preferred_element_type=jnp.float32)
    h_first = jax.nn.silu(z_first).astype(jnp.bfloat16)
    p_second = aggregate(h_first, stale_features, tile_val, tile_src).astype(jnp.bfloat16)
    layer_out = jnp.dot(p_second, w_second, preferred_element_type=jnp.float32).astype(jnp.bfloat16)
    upstream = lax.dot_general(
        out_grad, w_second, (((1,), (1,)), ((), ())), preferred_element_type=jnp.float32
    ).astype(jnp.bfloat16)
    g_second = lax.dot_general(
        p_second, out_grad, (((0,), (0,)), ((), ())), preferred_element_type=jnp.float32
    )
    up_blocks = upstream.reshape(blocks, edge, feature_width)
    slots = blocks + stale_features.shape[0] // edge
    spreads = jnp.zeros((slots, edge, feature_width), jnp.float32)
    for column in range(tiles_row):
        product = jnp.einsum(
            "rij,rif->rjf", tile_val[:, column], up_blocks, preferred_element_type=jnp.float32
        )
        spreads = spreads.at[tile_src[:, column]].add(product)
    spreads = spreads.reshape(-1, feature_width)
    local_part = spreads[:local_count]
    rim_part = spreads[local_count:].astype(jnp.bfloat16).reshape(peers, piece_rows, feature_width)
    joined = jnp.concatenate([outgoing(h_first), rim_part], 2)
    arrived = lax.all_to_all(joined, DOM, split_axis=0, concat_axis=0, tiled=True)
    fresh_features = arrived[:, :, :feature_width].reshape(-1, feature_width)
    fresh_grads = arrived[:, :, feature_width:].reshape(-1, feature_width)
    piece_count = local_count // piece_rows
    placing = (selects[:, None] == jnp.arange(piece_count, dtype=jnp.int32)[None, :]).astype(
        jnp.float32
    )
    stale_slots = stale_grads.reshape(peers, piece_rows, feature_width).astype(jnp.float32)
    placed = jnp.einsum("pq,prf->qrf", placing, stale_slots, precision=lax.Precision.HIGHEST)
    d_first = local_part + placed.reshape(-1, feature_width)
    sigma = jax.nn.sigmoid(z_first)
    dz = (d_first * sigma * (1.0 + z_first * (1.0 - sigma))).astype(jnp.bfloat16)
    g_first = lax.dot_general(
        p_first, dz, (((0,), (0,)), ((), ())), preferred_element_type=jnp.float32
    )
    grads = jnp.stack([g_first, g_second])
    shard = (
        summed_rows(grads.astype(jnp.bfloat16), (("dom_0", "dom_1"), ("dom_2", "grp")), 1)
        / total_nodes
    )
    moment_new = decay_first * moment_first + (1.0 - decay_first) * shard
    second_new = decay_second * moment_second + (1.0 - decay_second) * shard * shard
    update = (
        moment_new
        / (1.0 - decay_first**STEP)
        / (jnp.sqrt(second_new / (1.0 - decay_second**STEP)) + epsilon)
    )
    master_next = master - learn_rate * update
    rounded = master_next.astype(jnp.bfloat16)
    weights_next = whole_of(rounded, (("dom_0", "dom_1"), ("dom_2", "grp")), 1)
    return (layer_out, fresh_features, fresh_grads, master_next, weights_next)


def solution(mesh):
    torus = Mesh(
        mesh.devices.reshape(8, 4, 2, mesh.shape["grp"]), ("dom_0", "dom_1", "dom_2", "grp")
    )
    placed = (
        P(DOM_GRP, None),
        P(DOM_GRP, None),
        P(DOM_GRP, None, None, None),
        P(DOM_GRP, None),
        P(DOM_GRP, None),
        P(DOM_GRP, None),
        P(DOM_GRP, None),
        P(None, DOM_GRP, None),
        P(None, DOM_GRP, None),
        P(None, DOM_GRP, None),
    )
    return jax.shard_map(
        per_device,
        mesh=torus,
        in_specs=placed,
        out_specs=(
            P(DOM_GRP, None),
            P(DOM_GRP, None),
            P(DOM_GRP, None),
            P(None, DOM_GRP, None),
            P(),
        ),
        check_vma=False,
    )
```

profile of v0, /device:TPU:1, one launch (start us, length us, event | category | flops | bytes accessed | tf_op | source)
XLA Modules:
  0.0 310.1 jit_solution(5332855329391213524)
XLA Ops:
  2.2 11.9 %all-to-all-start.1 = ((bf16[32,2,2,512]{3,2,1,0:T(2,128)(2,1)}), bf16[32,2,2,512]{3,2,1,0:T(2,128)(2,1)S(1)}, u32[]{:S(2)}, u32[]{:S(2)}) async-start(bf16[32,2,2,512]{3,2,1,0:T(2,128)(2,1)} %broadcast_in_dim.22), calls=%async_computation.1 | async-start | bytes 262144 | tf_op jit(solution)/shard_map/all_to_all | solution.py:20
  16.2 7.2 %all-to-all-done.1 = bf16[32,2,2,512]{3,2,1,0:T(2,128)(2,1)S(1)} async-done(((bf16[32,2,2,512]{3,2,1,0:T(2,128)(2,1)}), bf16[32,2,2,512]{3,2,1,0:T(2,128)(2,1)S(1)}, u32[]{:S(2)}, u32[]{:S(2)}) %all-to-all-start.1) | async-done | bytes 131104 | tf_op jit(solution)/shard_map/all_to_all | solution.py:20
  24.5 6.5 %all-to-all-start.2 = ((bf16[8,32,2,2,512]{4,1,3,2,0:T(8,128)(2,1)}), bf16[8,32,2,2,512]{4,1,3,2,0:T(8,128)(2,1)}, u32[]{:S(2)}, u32[]{:S(2)}) async-start(bf16[8,32,2,2,512]{4,1,3,2,0:T(8,128)(2,1)} %broadcast_in_dim.23), calls=%async_computation.2 | async-start | bytes 2097152 | tf_op jit(solution)/shard_map/all_to_all | solution.py:20
  37.0 9.1 %all-to-all-done.2 = bf16[8,32,2,2,512]{4,1,3,2,0:T(8,128)(2,1)} async-done(((bf16[8,32,2,2,512]{4,1,3,2,0:T(8,128)(2,1)}), bf16[8,32,2,2,512]{4,1,3,2,0:T(8,128)(2,1)}, u32[]{:S(2)}, u32[]{:S(2)}) %all-to-all-start.2) | async-done | bytes 1048608 | tf_op jit(solution)/shard_map/all_to_all | solution.py:20
  46.1 5.9 %all-to-all-start = ((bf16[64,16,512]{2,1,0:T(8,128)(2,1)}), bf16[64,16,512]{2,1,0:T(8,128)(2,1)}, u32[]{:S(2)}, u32[]{:S(2)}) async-start(bf16[64,16,512]{2,1,0:T(8,128)(2,1)} %broadcast_select_fusion.1), calls=%async_computation | async-start | bytes 2097152 | tf_op jit(solution)/shard_map/all_to_all | solution.py:95
  60.2 2.9 copy.216
  69.7 2.9 copy.222
  74.5 2.9 copy.225
  79.3 2.9 copy.228
  84.2 2.9 copy.231
  98.2 4.9 %scatter_fusion = f32[16,128,512]{2,1,0:T(8,128)} fusion(f32[16,128,512]{2,1,0:T(8,128)} %broadcast_in_dim.24, s32[8]{0:T(128)S(1)} %get-tuple-element.20, f32[8,128,512]{2,1,0:T(8,128)} %copy.216), kind=kCustom, calls=%fused_computation.4 | custom fusion | flops 524288 | bytes 6291488 | tf_op jit(solution)/shard_map/scatter-add | solution.py:116
  103.1 4.9 %scatter_fusion.1 = f32[16,128,512]{2,1,0:T(8,128)} fusion(f32[16,128,512]{2,1,0:T(8,128)} %scatter_fusion, s32[8]{0:T(128)S(1)} %get-tuple-element.19, f32[8,128,512]{2,1,0:T(8,128)} %copy.219), kind=kCustom, calls=%fused_computation.5 | custom fusion | flops 524288 | bytes 6291488 | tf_op jit(solution)/shard_map/scatter-add | solution.py:116
  108.0 4.9 %scatter_fusion.2 = f32[16,128,512]{2,1,0:T(8,128)} fusion(f32[16,128,512]{2,1,0:T(8,128)} %scatter_fusion.1, s32[8]{0:T(128)S(1)} %get-tuple-element.18, f32[8,128,512]{2,1,0:T(8,128)} %copy.222), kind=kCustom, calls=%fused_computation.6 | custom fusion | flops 524288 | bytes 6291488 | tf_op jit(solution)/shard_map/scatter-add | solution.py:116
  112.9 5.3 %scatter_fusion.3 = f32[16,128,512]{2,1,0:T(8,128)} fusion(f32[16,128,512]{2,1,0:T(8,128)} %scatter_fusion.2, s32[8]{0:T(128)S(1)} %get-tuple-element.17, f32[8,128,512]{2,1,0:T(8,128)} %copy.225), kind=kCustom, calls=%fused_computation.7 | custom fusion | flops 524288 | bytes 6291488 | tf_op jit(solution)/shard_map/scatter-add | solution.py:116
  118.2 5.2 %scatter_fusion.4 = f32[16,128,512]{2,1,0:T(8,128)} fusion(f32[16,128,512]{2,1,0:T(8,128)} %scatter_fusion.3, s32[8]{0:T(128)S(1)} %get-tuple-element.21, f32[8,128,512]{2,1,0:T(8,128)} %copy.228), kind=kCustom, calls=%fused_computation.8 | custom fusion | flops 524288 | bytes 6291488 | tf_op jit(solution)/shard_map/scatter-add | solution.py:116
  123.4 5.0 %scatter_fusion.5 = f32[16,128,512]{2,1,0:T(8,128)} fusion(f32[16,128,512]{2,1,0:T(8,128)} %scatter_fusion.4, s32[8]{0:T(128)S(1)} %get-tuple-element.22, f32[8,128,512]{2,1,0:T(8,128)} %copy.231), kind=kCustom, calls=%fused_computation.9 | custom fusion | flops 524288 | bytes 6291488 | tf_op jit(solution)/shard_map/scatter-add | solution.py:116
  128.4 5.0 %scatter_fusion.6 = f32[16,128,512]{2,1,0:T(8,128)} fusion(f32[16,128,512]{2,1,0:T(8,128)} %scatter_fusion.5, s32[8]{0:T(128)S(1)} %get-tuple-element.23, f32[8,128,512]{2,1,0:T(8,128)} %copy.234), kind=kCustom, calls=%fused_computation.10 | custom fusion | flops 524288 | bytes 6291488 | tf_op jit(solution)/shard_map/scatter-add | solution.py:116
  133.4 4.4 %scatter_fusion.7 = f32[16,128,512]{2,1,0:T(8,128)} fusion(f32[16,128,512]{2,1,0:T(8,128)} %scatter_fusion.6, s32[8]{0:T(128)S(1)} %get-tuple-element.16, f32[8,128,512]{2,1,0:T(8,128)S(1)} %copy.237), kind=kCustom, calls=%fused_computation.11 | custom fusion | flops 524288 | bytes 6291488 | tf_op jit(solution)/shard_map/scatter-add | solution.py:116
  137.7 3.2 %slice.109 = f32[8,128,512]{2,1,0:T(8,128)} slice(f32[16,128,512]{2,1,0:T(8,128)} %scatter_fusion.7), slice={[0:8], [0:128], [0:512]} | slice | bytes 4194304 | tf_op jit(solution)/shard_map/slice | solution.py:118
  143.8 5.5 %gather_fusion = bf16[64,128,512]{2,1,0:T(8,128)(2,1)} fusion(bf16[16,128,512]{2,1,0:T(8,128)(2,1)S(1)} %bitcast.166, s32[1024]{0:T(1024)S(1)} %pad_clamp_fusion), kind=kCustom, calls=%fused_computation.2 | custom fusion | bytes 16777472 | tf_op jit(solution)/shard_map/gather | solution.py:63
  149.3 5.3 %bitcast_convert_fusion.1 = bf16[8,512,128]{1,2,0:T(8,128)(2,1)S(1)} fusion(bf16[8,8,128,128]{3,2,1,0:T(8,128)(2,1)} %param.14, bf16[8,8,128,512]{3,2,1,0:T(8,128)(2,1)} %bitcast.169), kind=kOutput, calls=%fused_computation.21 | convolution fusion | flops 1074266112 | bytes 11534336 | tf_op jit(solution)/shard_map/rtij,rtjf->rif/dot_general | solution.py:64
  155.9 4.7 %fusion.2 = (bf16[1024,512]{1,0:T(8,128)(2,1)}, bf16[1024,512]{1,0:T(8,128)(2,1)S(1)}) fusion(f32[64,16,512]{2,1,0:T(8,128)} %copy.240, f32[8,128,512]{2,1,0:T(8,128)} %slice.109, bf16[1024,512]{1,0:T(8,128)(2,1)S(1)} %bitcast.180, bf16[512,512]{1,0:T(8,128)(2,1)S(1)} %copy-done.13), kind=kOutput, calls=%fused_computation.19 | convolution fusion | flops 543162368 | bytes 7864320 | tf_op jit(solution)/shard_map/dot_general | solution.py:99
  161.6 5.5 %gather_fusion.1 = bf16[64,128,512]{2,1,0:T(8,128)(2,1)} fusion(bf16[16,128,512]{2,1,0:T(8,128)(2,1)S(1)} %bitcast.167, s32[1024]{0:T(1024)S(1)} %pad_clamp_fusion), kind=kCustom, calls=%fused_computation.3 | custom fusion | bytes 16777472 | tf_op jit(solution)/shard_map/gather | solution.py:63
  167.1 5.3 %bitcast_convert_fusion = bf16[8,512,128]{1,2,0:T(8,128)(2,1)S(1)} fusion(bf16[8,8,128,128]{3,2,1,0:T(8,128)(2,1)} %param.14, bf16[8,8,128,512]{3,2,1,0:T(8,128)(2,1)} %bitcast.168), kind=kOutput, calls=%fused_computation.20 | convolution fusion | flops 1074266112 | bytes 11534336 | tf_op jit(solution)/shard_map/rtij,rtjf->rif/dot_general | solution.py:64
  177.1 18.6 %all_to_all.40 = bf16[8,32,2,2,512]{4,3,1,2,0:T(2,128)(2,1)S(1)} all-to-all(bf16[8,32,2,2,512]{4,3,1,2,0:T(2,128)(2,1)S(1)} %bitcast.171), channel_id=1, replica_groups=mesh['dom_0'=8,'dom_1'=4,'dom_2'=2,'grp'=4] {'dom_2','grp'}, dimensions={0} | all-to-all | bytes 2097152 | tf_op jit(solution)/shard_map/all_to_all | solution.py:46
  197.0 18.8 %all_to_all.41 = bf16[32,2,2,512]{3,2,1,0:T(2,128)(2,1)S(1)} all-to-all(bf16[32,2,2,512]{3,2,1,0:T(2,128)(2,1)S(1)} %copy.244), channel_id=1, replica_groups=mesh['dom_0'=8,'dom_1'=4,'dom_2'=2,'grp'=4] {'dom_0','dom_1'}, dimensions={0} | all-to-all | bytes 262144 | tf_op jit(solution)/shard_map/all_to_all | solution.py:54
  216.6 13.0 %all_to_all.42 = bf16[32,2,2,512]{3,2,1,0:T(2,128)(2,1)S(1)} all-to-all(bf16[32,2,2,512]{3,2,1,0:T(2,128)(2,1)S(1)} %broadcast_in_dim.25), channel_id=1, replica_groups=mesh['dom_0'=8,'dom_1'=4,'dom_2'=2,'grp'=4] {'dom_0','dom_1'}, dimensions={0} | all-to-all | bytes 262144 | tf_op jit(solution)/shard_map/all_to_all | solution.py:20
  231.5 6.5 %all-to-all-start.7 = ((bf16[8,32,2,2,512]{4,3,1,2,0:T(2,128)(2,1)}), bf16[8,32,2,2,512]{4,3,1,2,0:T(2,128)(2,1)S(1)}, u32[]{:S(2)}, u32[]{:S(2)}) async-start(bf16[8,32,2,2,512]{4,3,1,2,0:T(2,128)(2,1)} %broadcast_in_dim.26), calls=%async_computation.7 | async-start | bytes 2097152 | tf_op jit(solution)/shard_map/all_to_all | solution.py:20
  244.2 8.8 %all-to-all-done.7 = bf16[8,32,2,2,512]{4,3,1,2,0:T(2,128)(2,1)S(1)} async-done(((bf16[8,32,2,2,512]{4,3,1,2,0:T(2,128)(2,1)}), bf16[8,32,2,2,512]{4,3,1,2,0:T(2,128)(2,1)S(1)}, u32[]{:S(2)}, u32[]{:S(2)}) %all-to-all-start.7) | async-done | bytes 1048608 | tf_op jit(solution)/shard_map/all_to_all | solution.py:20
  254.0 4.5 %all-to-all-start.3 = ((bf16[64,16,1024]{2,1,0:T(8,128)(2,1)}), bf16[64,16,1024]{2,1,0:T(8,128)(2,1)S(1)}, u32[]{:S(2)}, u32[]{:S(2)}) async-start(bf16[64,16,1024]{2,1,0:T(8,128)(2,1)} %pad_maximum_fusion.2), calls=%async_computation.3 | async-start | bytes 4194304 | tf_op jit(solution)/shard_map/all_to_all | solution.py:121
  258.5 3.1 %convolution_convert_fusion.1 = bf16[1024,512]{1,0:T(8,128)(2,1)} fusion(bf16[1024,512]{1,0:T(8,128)(2,1)} %bitcast.178, bf16[512,512]{1,0:T(8,128)(2,1)} %squeeze.43), kind=kOutput, calls=%fused_computation.33 | convolution fusion | flops 537395200 | bytes 2621440 | tf_op jit(solution)/shard_map/dot_general | solution.py:102
  264.4 43.7 %all-to-all-done.3 = bf16[64,16,1024]{2,1,0:T(8,128)(2,1)S(1)} async-done(((bf16[64,16,1024]{2,1,0:T(8,128)(2,1)}), bf16[64,16,1024]{2,1,0:T(8,128)(2,1)S(1)}, u32[]{:S(2)}, u32[]{:S(2)}) %all-to-all-start.3) | async-done | bytes 2097184 | tf_op jit(solution)/shard_map/all_to_all | solution.py:121
  (101 shorter events, 67.5 us)
Async XLA Ops:
  0.6 13.4 %copy-start = (bf16[1024,512]{1,0:T(8,128)(2,1)S(1)}, bf16[1024,512]{1,0:T(8,128)(2,1)}, u32[]{:S(2)}) copy-start(bf16[1024,512]{1,0:T(8,128)(2,1)} %param.17) | copy-start | bytes 3145732
  0.6 15.5 %copy-start.14 = (s32[8,8]{1,0:T(8,128)S(1)}, s32[8,8]{1,0:T(8,128)}, u32[]{:S(2)}) copy-start(s32[8,8]{1,0:T(8,128)} %param.13) | copy-start | bytes 772
  2.2 21.2 %all-to-all-start.1 = ((bf16[32,2,2,512]{3,2,1,0:T(2,128)(2,1)}), bf16[32,2,2,512]{3,2,1,0:T(2,128)(2,1)S(1)}, u32[]{:S(2)}, u32[]{:S(2)}) async-start(bf16[32,2,2,512]{3,2,1,0:T(2,128)(2,1)} %broadcast_in_dim.22), calls=%async_computation.1 | async-start | bytes 262144 | tf_op jit(solution)/shard_map/all_to_all | solution.py:20
  16.2 14.9 %copy-start.18 = (s32[1,64]{1,0:T(1,128)S(1)}, s32[1,64]{1,0:T(1,128)}, u32[]{:S(2)}) copy-start(s32[1,64]{1,0:T(1,128)} %param.15) | copy-start | bytes 772
  24.5 21.6 %all-to-all-start.2 = ((bf16[8,32,2,2,512]{4,1,3,2,0:T(8,128)(2,1)}), bf16[8,32,2,2,512]{4,1,3,2,0:T(8,128)(2,1)}, u32[]{:S(2)}, u32[]{:S(2)}) async-start(bf16[8,32,2,2,512]{4,1,3,2,0:T(8,128)(2,1)} %broadcast_in_dim.23), calls=%async_computation.2 | async-start | bytes 2097152 | tf_op jit(solution)/shard_map/all_to_all | solution.py:20
  46.1 96.3 %all-to-all-start = ((bf16[64,16,512]{2,1,0:T(8,128)(2,1)}), bf16[64,16,512]{2,1,0:T(8,128)(2,1)}, u32[]{:S(2)}, u32[]{:S(2)}) async-start(bf16[64,16,512]{2,1,0:T(8,128)(2,1)} %broadcast_select_fusion.1), calls=%async_computation | async-start | bytes 2097152 | tf_op jit(solution)/shard_map/all_to_all | solution.py:95
  55.3 3.1 %copy-start.2 = (bf16[8,8,128,128]{3,2,1,0:T(8,128)(2,1)S(1)}, bf16[8,8,128,128]{3,2,1,0:T(8,128)(2,1)}, u32[]{:S(2)}) copy-start(bf16[8,8,128,128]{3,2,1,0:T(8,128)(2,1)} %param.14) | copy-start | bytes 6291460
  137.7 3.2 %copy-start.10 = (bf16[1,256,2,512]{3,1,2,0:T(8,128)(2,1)S(1)}, bf16[1,256,2,512]{3,1,2,0:T(8,128)(2,1)}, u32[]{:S(2)}) copy-start(bf16[1,256,2,512]{3,1,2,0:T(8,128)(2,1)} %get-tuple-element.31) | copy-start | bytes 1572868
  140.9 1.5 copy-start.5
  154.6 1.3 copy-start.13
  155.9 4.7 %copy-start.12 = (bf16[1024,512]{1,0:T(8,128)(2,1)S(1)}, bf16[1024,512]{1,0:T(8,128)(2,1)}, u32[]{:S(2)}) copy-start(bf16[1024,512]{1,0:T(8,128)(2,1)} %param.16) | copy-start | bytes 3145732
  160.6 1.0 copy-start.6
  172.4 2.3 copy-start.9
  172.4 1.6 copy-start.19
  173.2 1.6 copy-start.11
  173.2 1.6 copy-start.20
  177.0 38.8 %copy-start.15 = (f32[2,2,512]{2,1,0:T(2,128)S(1)}, f32[2,2,512]{2,1,0:T(2,128)}, u32[]{:S(2)}) copy-start(f32[2,2,512]{2,1,0:T(2,128)} %param.19) | copy-start | bytes 24580
  177.1 38.8 %copy-start.16 = (f32[2,2,512]{2,1,0:T(2,128)S(1)}, f32[2,2,512]{2,1,0:T(2,128)}, u32[]{:S(2)}) copy-start(f32[2,2,512]{2,1,0:T(2,128)} %param.21) | copy-start | bytes 24580
  177.1 38.8 %copy-start.17 = (f32[2,2,512]{2,1,0:T(2,128)S(1)}, f32[2,2,512]{2,1,0:T(2,128)}, u32[]{:S(2)}) copy-start(f32[2,2,512]{2,1,0:T(2,128)} %param.20) | copy-start | bytes 24580
  231.5 9.2 %copy-start.7 = (bf16[1024,512]{1,0:T(8,128)(2,1)S(1)}, bf16[1024,512]{1,0:T(8,128)(2,1)}, u32[]{:S(2)}) copy-start(bf16[1024,512]{1,0:T(8,128)(2,1)} %copy-done.6) | copy-start | bytes 3145732
  231.5 21.5 %all-to-all-start.7 = ((bf16[8,32,2,2,512]{4,3,1,2,0:T(2,128)(2,1)}), bf16[8,32,2,2,512]{4,3,1,2,0:T(2,128)(2,1)S(1)}, u32[]{:S(2)}, u32[]{:S(2)}) async-start(bf16[8,32,2,2,512]{4,3,1,2,0:T(2,128)(2,1)} %broadcast_in_dim.26), calls=%async_computation.7 | async-start | bytes 2097152 | tf_op jit(solution)/shard_map/all_to_all | solution.py:20
  241.3 1.2 copy-start.8
  253.0 1.0 copy-start.3
  254.0 54.2 %all-to-all-start.3 = ((bf16[64,16,1024]{2,1,0:T(8,128)(2,1)}), bf16[64,16,1024]{2,1,0:T(8,128)(2,1)S(1)}, u32[]{:S(2)}, u32[]{:S(2)}) async-start(bf16[64,16,1024]{2,1,0:T(8,128)(2,1)} %pad_maximum_fusion.2), calls=%async_computation.3 | async-start | bytes 4194304 | tf_op jit(solution)/shard_map/all_to_all | solution.py:121
  258.5 3.1 %copy-start.4 = (bf16[8,32,2,2,512]{4,3,1,2,0:T(2,128)(2,1)S(1)}, bf16[8,32,2,2,512]{4,3,1,2,0:T(2,128)(2,1)}, u32[]{:S(2)}) copy-start(bf16[8,32,2,2,512]{4,3,1,2,0:T(2,128)(2,1)} %copy-done.3) | copy-start | bytes 3145732
  263.3 46.5 %copy-start.1 = (bf16[1024,512]{1,0:T(8,128)(2,1)S(1)}, bf16[1024,512]{1,0:T(8,128)(2,1)}, u32[]{:S(2)}) copy-start(bf16[1024,512]{1,0:T(8,128)(2,1)} %param.17) | copy-start | bytes 3145732
where the time goes:
time: 316 us; the launch traced here: 310 us
  waiting for transfers between devices  68.9 us (22%)
  local copies, waits for them, and re-layouts  68.2 us (22%)
  blocking collectives  50.4 us (16%)
  other arithmetic  47.1 us (15%)
  matrix products  38.9 us (12%)
  starting transfers between devices  35.3 us (11%)
    all_to_all x1, waiting for transfers between devices, per_device(): lax.all_to_all(joined, DOM, split_axis=0, concat_axis=0, tiled=True)  43.7 us
    scatter-add x8, other arithmetic, per_device(): spreads = spreads.at[tile_src[:, column]].add(product)  39.5 us
    all_to_all x3, waiting for transfers between devices, from_everyone(): lax.all_to_all(jnp.broadcast_to(array[None], (peers, *array.shape)), axis...  25.2 us
    all_to_all x3, starting transfers between devices, from_everyone(): lax.all_to_all(jnp.broadcast_to(array[None], (peers, *array.shape)), axis...  24.9 us
    dot_general x8, local copies, waits for them, and re-layouts, per_device(): jnp.einsum('rij,rif->rjf', tile_val[:, column], up_blocks, preferred_elem...  22.3 us
    all_to_all x1, blocking collectives, summed_rows(): lax.all_to_all(nearer.astype(jnp.bfloat16), far, split_axis=0, concat_axi...  18.8 us
    all_to_all x1, blocking collectives, sent_and_summed(): lax.all_to_all(tiles, axis, split_axis=0, concat_axis=0, tiled=True)  18.6 us
    dot_general x8, matrix products, per_device(): jnp.einsum('rij,rif->rjf', tile_val[:, column], up_blocks, preferred_elem...  15 us
  transfers between devices with their start and end apart: 5, of which 4 were waited for; matrix products, arithmetic and copies ran while one was open for 35% of the time, Pallas kernels for 0%

commit v1 on v0

v1 whole, which is shorter than its diff:
```python
import functools

import jax
import jax.numpy as jnp
from jax import lax
from jax.experimental import pallas as pl
from jax.experimental.pallas import tpu as pltpu
from jax.sharding import Mesh
from jax.sharding import PartitionSpec as P

STEP = 10
DEVICES = ("z", "x", "c", "y")
NZ, NX, NC, NY = 8, 4, 2, 4
PEERS = NZ * NX * NC
F = 512
NODES = 1024
PIECE = 16
TOTAL_NODES = 262144
MESH = pl.DeviceIdType.MESH
BF16 = jnp.bfloat16
F32 = jnp.float32

decay_first = 0.9
decay_second = 0.95
learn_rate = 0.01
epsilon = 1e-08


def dot(a, b):
    return jnp.dot(a, b, preferred_element_type=F32)


def dot_over_rows(a, b):
    return lax.dot_general(a, b, (((0,), (0,)), ((), ())), preferred_element_type=F32)


def dot_over_columns(a, b):
    return lax.dot_general(a, b, (((1,), (1,)), ((), ())), preferred_element_type=F32)


def rows_of(index, count):
    return pl.ds(pl.multiple_of(index * count, count), count)


def repeat(count, body):
    def step(i, carry):
        body(i)
        return carry

    lax.fori_loop(0, count, step, 0)


def kernel(
    src_ref,
    sel_row_ref,
    master_ref,
    first_ref,
    second_ref,
    features_hbm,
    tiles_hbm,
    stale_features_hbm,
    stale_grads_hbm,
    out_grad_hbm,
    layer_out_hbm,
    fresh_features_hbm,
    fresh_grads_hbm,
    master_next_ref,
    weights_next_hbm,
    features,
    rim,
    tiles,
    dense,
    out_grad,
    stale_features,
    stale_grads,
    raw_send,
    feature_send,
    grad_send,
    upstream,
    p_local,
    p_stale,
    d_first,
    p_first,
    dz,
    hidden,
    p_second,
    layer_out,
    weights,
    weights_next,
    gather_now,
    gather_next,
    grad_blocks,
    from_core,
    core_sum,
    from_y,
    y_sum,
    from_plane,
    shard_now,
    shard_next,
    rows_f32,
    src_wide,
    want_down,
    choose,
    perm,
    perm_back,
    load_sem,
    store_sem,
    send_sem,
    recv_sem,
):
    z, x, c, y = (lax.axis_index(a) for a in DEVICES)
    plane = z * NX + x
    me = plane * NC + c

    loads = [
        pltpu.make_async_copy(s, d, load_sem.at[i])
        for i, (s, d) in enumerate(
            (
                (features_hbm, features),
                (tiles_hbm, tiles),
                (out_grad_hbm, out_grad),
                (stale_grads_hbm, stale_grads),
                (stale_features_hbm, stale_features),
            )
        )
    ]
    for load in loads:
        load.start()

    def peer_at(step):
        dz_, dx_, dc_ = step // 8, (step // 2) % 4, step % 2
        return ((z + dz_) % NZ, (x + dx_) % NX, (c + dc_) % NC)

    def plane_at(step):
        return ((z + step // 4) % NZ, (x + step % 4) % NX)

    barrier = pltpu.get_barrier_semaphore()

    def greet(i):
        pz, px, pc = peer_at(i + 1)
        pl.semaphore_signal(barrier, inc=1, device_id=(pz, px, pc, y), device_id_type=MESH)

    repeat(PEERS - 1, greet)
    for k in range(1, NY):
        pl.semaphore_signal(
            barrier, inc=1, device_id=(z, x, c, (y + k) % NY), device_id_type=MESH
        )

    def fill_rows(target, source):
        for m in range(2):
            for r in range(2):
                for j in range(4):
                    s = m * 8 + r * 4 + j
                    target[s : s + 1, :] = source[m, r : r + 1, j * 128 : (j + 1) * 128]

    fill_rows(rows_f32.at[0], master_ref)
    fill_rows(rows_f32.at[1], first_ref)
    fill_rows(rows_f32.at[2], second_ref)
    shard_now[...] = rows_f32[0].astype(BF16)

    def bits(o):
        m, j, p = o >> 7, (o >> 5) & 3, (o >> 4) & 1
        return (((o >> 3) & 1) << 7) | (((o >> 1) & 3) << 5) | (p << 4) | (m << 3) | ((o & 1) << 2) | j

    down = lax.broadcasted_iota(jnp.int32, (256, 256), 0)
    along = lax.broadcasted_iota(jnp.int32, (256, 256), 1)
    perm[...] = (bits(down) == along).astype(F32).astype(BF16)
    perm_back[...] = (bits(along) == down).astype(F32).astype(BF16)

    slot_of = lax.broadcasted_iota(jnp.int32, (PEERS, NODES), 1) // PIECE
    slot_at = lax.broadcasted_iota(jnp.int32, (PEERS, NODES), 0)
    widen = (slot_of == slot_at).astype(F32).astype(BF16)
    picks = jnp.broadcast_to(sel_row_ref[...].astype(F32), (16, PEERS)).astype(BF16)
    wide = dot(picks, widen)[0:1, :].astype(jnp.int32)
    lane = lax.broadcasted_iota(jnp.int32, (1, NODES), 1) % PIECE
    wanted = wide * PIECE + lane

    tall = dot_over_rows(widen, dot_over_rows(picks, jnp.full((16, 128), 0.0625, BF16)).astype(BF16))
    want_down[...] = tall.astype(jnp.int32) * PIECE + (
        lax.broadcasted_iota(jnp.int32, (NODES, 128), 0) % PIECE
    )

    def choose_rows(i):
        rows = rows_of(i, 256)
        for k in range(8):
            column = lax.broadcasted_iota(jnp.int32, (256, 128), 1) + k * 128
            chosen = (want_down[rows, :] == column).astype(F32).astype(BF16)
            choose[rows, k * 128 : (k + 1) * 128] = chosen

    repeat(4, choose_rows)

    pl.semaphore_wait(barrier, PEERS - 1 + NY - 1)

    def spread_shard(slot, shard, gathered):
        gathered[c, y, rows_of(plane, 16), :] = shard[...]

        def send(i):
            pz, px = plane_at(i + 1)
            pltpu.make_async_remote_copy(
                src_ref=shard,
                dst_ref=gathered.at[c, y, rows_of(plane, 16)],
                send_sem=send_sem.at[slot],
                recv_sem=recv_sem.at[slot],
                device_id=(pz, px, c, y),
                device_id_type=MESH,
            ).start()

        repeat(NZ * NX - 1, send)

    def plane_bytes(slot, ref):
        return pltpu.make_async_remote_copy(
            src_ref=ref,
            dst_ref=ref,
            send_sem=send_sem.at[slot],
            recv_sem=recv_sem.at[slot],
            device_id=(z, x, c, (y + 1) % NY),
            device_id_type=MESH,
        )

    def gather_y(slot, gathered):
        plane_bytes(slot, gathered.at[0, 0, pl.ds(0, 496)]).wait_recv()
        copies = [
            pltpu.make_async_remote_copy(
                src_ref=gathered.at[c, y],
                dst_ref=gathered.at[c, y],
                send_sem=send_sem.at[slot + 1],
                recv_sem=recv_sem.at[slot + 1],
                device_id=(z, x, c, (y + k) % NY),
                device_id_type=MESH,
            )
            for k in range(1, NY)
        ]
        for copy in copies:
            copy.start()

    def gather_core(slot, gathered):
        plane_bytes(slot + 1, gathered.at[0, pl.ds(0, 3)]).wait_recv()
        pltpu.make_async_remote_copy(
            src_ref=gathered.at[c],
            dst_ref=gathered.at[c],
            send_sem=send_sem.at[slot + 2],
            recv_sem=recv_sem.at[slot + 2],
            device_id=(z, x, 1 - c, y),
            device_id_type=MESH,
        ).start()

    def gather_end(slot, gathered, whole):
        plane_bytes(slot + 2, gathered.at[0]).wait_recv()

        def lay(chunk):
            taken = jnp.concatenate(
                [gathered[a // 4, a % 4, rows_of(chunk, 32), :] for a in range(8)], 0
            )
            laid = dot(perm[...], taken).astype(BF16)
            for m in range(2):
                for j in range(4):
                    at = (m * 4 + j) * 32
                    whole[m, rows_of(chunk, 32), j * 128 : (j + 1) * 128] = laid[at : at + 32]

        repeat(16, lay)

    def pick_pieces(target, table):
        def pick(i):
            rows = rows_of(i, 256)
            target[rows, :] = dot(choose[rows, :], table[...]).astype(BF16)

        repeat(4, pick)

    def send_pieces(slot, source, target):
        def send(i):
            pz, px, pc = peer_at(i + 1)
            peer = (pz * NX + px) * NC + pc
            pltpu.make_async_remote_copy(
                src_ref=source.at[rows_of(peer, PIECE)],
                dst_ref=target.at[rows_of(me, PIECE)],
                send_sem=send_sem.at[slot],
                recv_sem=recv_sem.at[slot],
                device_id=(pz, px, pc, y),
                device_id_type=MESH,
            ).start()

        repeat(PEERS - 1, send)

    sent_bytes = pl.ds(0, (PEERS - 1) * PIECE)

    spread_shard(0, shard_now, gather_now)
    loads[0].wait()
    pick_pieces(raw_send, features)
    send_pieces(3, raw_send, rim)
    rim[rows_of(me, PIECE), :] = raw_send[rows_of(me, PIECE), :]

    tile_of = lax.broadcasted_iota(jnp.int32, (8, 1024), 1) // 128
    tile_at = lax.broadcasted_iota(jnp.int32, (8, 1024), 0)
    wide_ids = dot(src_ref[...].astype(F32), (tile_of == tile_at).astype(F32))
    for i in range(8):
        src_wide[i * 8 : (i + 1) * 8, :] = jnp.broadcast_to(wide_ids[i : i + 1, :], (8, 1024))
    loads[1].wait()

    def densify(i):
        def column(b):
            target = jnp.full((8, 128), b, jnp.int32).astype(F32)
            total = jnp.zeros((128, 128), F32)
            for t in range(8):
                ids = src_wide[rows_of(i, 8), t * 128 : (t + 1) * 128]
                chosen = (ids == target).astype(F32)[0:1, :]
                total = total + tiles[i, t].astype(F32) * chosen
            dense[rows_of(i, 128), rows_of(b, 128)] = total.astype(BF16)

        repeat(16, column)

    repeat(3, densify)
    gather_y(0, gather_now)
    repeat(3, lambda i: densify(i + 3))
    gather_core(0, gather_now)
    repeat(2, lambda i: densify(i + 6))

    loads[2].wait()
    gather_end(0, gather_now, weights)

    def up(i):
        rows = rows_of(i, 256)
        upstream[rows, :] = dot_over_columns(out_grad[rows, :], weights[1]).astype(BF16)

    repeat(4, up)

    def rim_part(i):
        part = dot_over_rows(dense[:, rows_of(i + 4, 256)], upstream[...])
        grad_send[rows_of(i, 256), :] = part.astype(BF16)

    repeat(4, rim_part)
    send_pieces(4, grad_send, fresh_grads_hbm)
    own_grads = pltpu.make_async_copy(
        grad_send.at[rows_of(me, PIECE)], fresh_grads_hbm.at[rows_of(me, PIECE)], store_sem.at[0]
    )
    own_grads.start()

    loads[3].wait()
    loads[4].wait()
    def local_part(i):
        rows = rows_of(i, 256)
        row = lax.broadcasted_iota(jnp.int32, (256, NODES), 0) + i * 256
        placing = (row == wanted).astype(F32).astype(BF16)
        d_first[rows, :] = dot_over_rows(dense[:, rows], upstream[...]) + dot(
            placing, stale_grads[...]
        )

    repeat(4, local_part)

    def ahead(i):
        rows = rows_of(i, 256)
        p_local[rows, :] = dot(dense[rows, 0:NODES], features[...])
        p_stale[rows, :] = dot(dense[rows, NODES : 2 * NODES], stale_features[...])

    repeat(4, ahead)

    plane_bytes(3, rim.at[sent_bytes]).wait_recv()

    def first_layer(i):
        rows = rows_of(i, 256)
        p = (p_local[rows, :] + dot(dense[rows, NODES : 2 * NODES], rim[...])).astype(BF16)
        p_first[rows, :] = p
        zf = dot(p, weights[0])
        s = 1.0 / (1.0 + jnp.exp(-zf))
        hidden[rows, :] = (zf * s).astype(BF16)
        dz[rows, :] = (d_first[rows, :] * s * (1.0 + zf * (1.0 - s))).astype(BF16)

    repeat(4, first_layer)
    pick_pieces(feature_send, hidden)
    send_pieces(5, feature_send, fresh_features_hbm)
    own_features = pltpu.make_async_copy(
        feature_send.at[rows_of(me, PIECE)],
        fresh_features_hbm.at[rows_of(me, PIECE)],
        store_sem.at[1],
    )
    own_features.start()

    def second_layer(i):
        rows = rows_of(i, 256)
        p_second[rows, :] = (p_stale[rows, :] + dot(dense[rows, 0:NODES], hidden[...])).astype(BF16)

    repeat(4, second_layer)

    def grad_rows(i):
        chunk = 8
        first = dot_over_rows(p_first[:, rows_of(i, 256)], dz[...]).astype(BF16)
        second = dot_over_rows(p_second[:, rows_of(i, 256)], out_grad[...]).astype(BF16)
        for k in range(chunk):
            stacked = jnp.concatenate(
                [
                    g[k * 32 : (k + 1) * 32, j * 128 : (j + 1) * 128]
                    for g in (first, second)
                    for j in range(4)
                ],
                0,
            )
            blocks = dot(perm_back[...], stacked).astype(BF16)
            for a in range(8):
                grad_blocks[a // 4, a % 4, rows_of(i * chunk + k, 32), :] = blocks[
                    a * 32 : (a + 1) * 32
                ]

    repeat(2, grad_rows)

    pltpu.make_async_remote_copy(
        src_ref=grad_blocks.at[1 - c],
        dst_ref=from_core,
        send_sem=send_sem.at[6],
        recv_sem=recv_sem.at[6],
        device_id=(z, x, 1 - c, y),
        device_id_type=MESH,
    ).start()

    def last(i):
        rows = rows_of(i, 256)
        layer_out[rows, :] = dot(p_second[rows, :], weights[1]).astype(BF16)

    repeat(4, last)
    store_layer = pltpu.make_async_copy(layer_out, layer_out_hbm, store_sem.at[2])
    store_layer.start()

    plane_bytes(6, from_core).wait_recv()
    for k in range(NY):
        core_sum[k] = (grad_blocks[c, k].astype(F32) + from_core[k].astype(F32)).astype(BF16)
    for k in range(1, NY):
        pltpu.make_async_remote_copy(
            src_ref=core_sum.at[(y + k) % NY],
            dst_ref=from_y.at[k - 1],
            send_sem=send_sem.at[7],
            recv_sem=recv_sem.at[7],
            device_id=(z, x, c, (y + k) % NY),
            device_id_type=MESH,
        ).start()
    plane_bytes(7, from_y).wait_recv()
    y_sum[...] = (
        core_sum[y].astype(F32)
        + from_y[0].astype(F32)
        + from_y[1].astype(F32)
        + from_y[2].astype(F32)
    ).astype(BF16)
    from_plane[rows_of(plane, 16), :] = y_sum[rows_of(plane, 16), :]

    def send_shard(i):
        pz, px = plane_at(i + 1)
        pltpu.make_async_remote_copy(
            src_ref=y_sum.at[rows_of(pz * NX + px, 16)],
            dst_ref=from_plane.at[rows_of(plane, 16)],
            send_sem=send_sem.at[8],
            recv_sem=recv_sem.at[8],
            device_id=(pz, px, c, y),
            device_id_type=MESH,
        ).start()

    repeat(NZ * NX - 1, send_shard)
    plane_bytes(8, from_plane.at[pl.ds(0, 496)]).wait_recv()
    total = from_plane[0:16, :].astype(F32)
    for k in range(1, NZ * NX):
        total = total + from_plane[k * 16 : (k + 1) * 16, :].astype(F32)
    grads = total / TOTAL_NODES
    moment_new = decay_first * rows_f32[1] + (1.0 - decay_first) * grads
    second_new = decay_second * rows_f32[2] + (1.0 - decay_second) * grads * grads
    update = (
        moment_new
        / (1.0 - decay_first**STEP)
        / (jnp.sqrt(second_new / (1.0 - decay_second**STEP)) + epsilon)
    )
    master_next = rows_f32[0] - learn_rate * update
    rows_f32[3] = master_next
    shard_next[...] = master_next.astype(BF16)
    spread_shard(9, shard_next, gather_next)
    for m in range(2):
        for r in range(2):
            for j in range(4):
                s = m * 8 + r * 4 + j
                master_next_ref[m, r : r + 1, j * 128 : (j + 1) * 128] = rows_f32[3, s : s + 1, :]
    gather_y(9, gather_next)
    gather_core(9, gather_next)
    gather_end(9, gather_next, weights_next)
    store_weights = pltpu.make_async_copy(weights_next, weights_next_hbm, store_sem.at[3])
    store_weights.start()

    for slot, shard, gathered in ((0, gather_now, gather_now), (9, gather_next, gather_next)):
        plane_bytes(slot, gathered.at[0, 0, pl.ds(0, 496)]).wait_send()
        plane_bytes(slot + 1, gathered.at[0, pl.ds(0, 3)]).wait_send()
        plane_bytes(slot + 2, gathered.at[0]).wait_send()
    plane_bytes(6, from_core).wait_send()
    plane_bytes(7, from_y).wait_send()
    plane_bytes(8, from_plane.at[pl.ds(0, 496)]).wait_send()
    for slot, source in ((3, raw_send), (4, grad_send), (5, feature_send)):
        plane_bytes(slot, source.at[sent_bytes]).wait_send()
    plane_bytes(4, fresh_grads_hbm.at[sent_bytes]).wait_recv()
    plane_bytes(5, fresh_features_hbm.at[sent_bytes]).wait_recv()
    own_grads.wait()
    own_features.wait()
    store_layer.wait()
    store_weights.wait()


def per_device(
    features,
    tile_src,
    tile_val,
    send_sel,
    stale_features,
    stale_grads,
    out_grad,
    master,
    moment_first,
    moment_second,
):
    any_space = pl.BlockSpec(memory_space=pl.ANY)
    vmem = pl.BlockSpec(memory_space=pltpu.VMEM)
    nodes = pltpu.VMEM((NODES, F), BF16)
    nodes_f32 = pltpu.VMEM((NODES, F), F32)
    matrices = pltpu.VMEM((2, F, F), BF16)
    blocks = pltpu.VMEM((2, NY, 512, 128), BF16)
    half = pltpu.VMEM((NY, 512, 128), BF16)
    lines = pltpu.VMEM((512, 128), BF16)
    shard = pltpu.VMEM((16, 128), BF16)
    square = pltpu.VMEM((256, 256), BF16)
    rows = jax.ShapeDtypeStruct((NODES, F), BF16)
    return pl.pallas_call(
        kernel,
        out_shape=(
            rows,
            rows,
            rows,
            jax.ShapeDtypeStruct((2, 2, F), F32),
            jax.ShapeDtypeStruct((2, F, F), BF16),
        ),
        in_specs=[vmem, vmem, vmem, vmem, vmem] + [any_space] * 5,
        out_specs=(any_space, any_space, any_space, vmem, any_space),
        scratch_shapes=[
            nodes,
            nodes,
            pltpu.VMEM((8, 8, 128, 128), BF16),
            pltpu.VMEM((NODES, 2 * NODES), BF16),
            nodes,
            nodes,
            nodes,
            nodes,
            nodes,
            nodes,
            nodes,
            nodes_f32,
            nodes_f32,
            nodes_f32,
            nodes,
            nodes,
            nodes,
            nodes,
            nodes,
            matrices,
            matrices,
            blocks,
            blocks,
            blocks,
            half,
            half,
            pltpu.VMEM((NY - 1, 512, 128), BF16),
            lines,
            lines,
            shard,
            shard,
            pltpu.VMEM((4, 16, 128), F32),
            pltpu.VMEM((64, 1024), F32),
            pltpu.VMEM((NODES, 128), jnp.int32),
            pltpu.VMEM((NODES, NODES), BF16),
            square,
            square,
            pltpu.SemaphoreType.DMA((5,)),
            pltpu.SemaphoreType.DMA((4,)),
            pltpu.SemaphoreType.DMA((12,)),
            pltpu.SemaphoreType.DMA((12,)),
        ],
        compiler_params=pltpu.CompilerParams(
            collective_id=0, has_side_effects=True, vmem_limit_bytes=56 * 2**20
        ),
        cost_estimate=pl.CostEstimate(
            flops=12 * 2**30, bytes_accessed=12 * 2**20, transcendentals=2**20
        ),
    )(
        tile_src,
        send_sel,
        master,
        moment_first,
        moment_second,
        features,
        tile_val,
        stale_features,
        stale_grads,
        out_grad,
    )


def solution(mesh):
    torus = Mesh(mesh.devices.reshape(NZ, NX, NC, NY), DEVICES)
    nodes = P(DEVICES, None)
    parts = P(None, DEVICES, None)
    return jax.shard_map(
        per_device,
        mesh=torus,
        in_specs=(
            nodes,
            nodes,
            P(DEVICES, None, None, None),
            nodes,
            nodes,
            nodes,
            nodes,
            parts,
            parts,
            parts,
        ),
        out_specs=(nodes, nodes, nodes, parts, P()),
        check_vma=False,
    )
```

time: 316 us -> 120 us (0.38); the launches traced: 310 us -> 120 us
  Pallas kernels: 0 us -> 113 us
  waiting for transfers between devices: 68.9 us -> 0 us
  local copies, waits for them, and re-layouts: 68.2 us -> 5.93 us
  blocking collectives: 50.4 us -> 0 us
  other arithmetic: 47.1 us -> 0 us
  matrix products: 38.9 us -> 0 us
  starting transfers between devices: 35.3 us -> 0 us
    pallas_call x0 -> x1, Pallas kernels: none -> 113 us  [per_device(): pl.pallas_call(kernel, out_shape=(rows, rows, rows, jax.ShapeDtypeStruct(...]
    all_to_all x5 -> x0, waiting for transfers between devices: 68.9 us -> none  [the longest x1 43.7 us: per_device(): lax.all_to_all(joined, DOM, split_axis=0, concat_axis=0, tiled=True)]
    all_to_all x3 -> x0, blocking collectives: 50.4 us -> none  [the longest x1 18.8 us: summed_rows(): lax.all_to_all(nearer.astype(jnp.bfloat16), far, split_axis=0, concat_axi...]
    scatter-add x8 -> x0, other arithmetic: 39.5 us -> none  [per_device(): spreads = spreads.at[tile_src[:, column]].add(product)]
    dot_general x16 -> x0, matrix products: 38.9 us -> none  [the longest x8 15 us: per_device(): jnp.einsum('rij,rif->rjf', tile_val[:, column], up_blocks, preferred_elem...]
    all_to_all x5 -> x0, starting transfers between devices: 35.3 us -> none  [the longest x3 24.9 us: from_everyone(): lax.all_to_all(jnp.broadcast_to(array[None], (peers, *array.shape)), axis...]
    dot_general x11 -> x0, local copies, waits for them, and re-layouts: 27 us -> none  [the longest x8 22.3 us: per_device(): jnp.einsum('rij,rif->rjf', tile_val[:, column], up_blocks, preferred_elem...]
    gather x4 -> x0, local copies, waits for them, and re-layouts: 13.5 us -> none  [the longest x2 11 us: aggregate(): picked = lookup[tile_src]]
  transfers between devices with their start and end apart: 5 -> 0, of which waited for: 4 -> 0; matrix products, arithmetic and copies ran while one was open for 35% -> 0% of each run, Pallas kernels for 0% -> 0%
where the time goes in v1:
time: 120 us
  Pallas kernels  113 us (94%)
  local copies, waits for them, and re-layouts  5.93 us (5%)
    pallas_call x1, Pallas kernels, per_device(): pl.pallas_call(kernel, out_shape=(rows, rows, rows, jax.ShapeDtypeStruct(...  113 us
    unnamed x13, local copies, waits for them, and re-layouts  5.93 us

profile of v1, /device:TPU:1, one launch (start us, length us, event | category | flops | bytes accessed | tf_op | source)
XLA Modules:
  0.0 119.9 jit_solution(9881459401922054515)
XLA Ops:
  0.6 113.3 %shard_map.137 = (bf16[1024,512]{1,0:T(8,128)(2,1)}, bf16[1024,512]{1,0:T(8,128)(2,1)}, bf16[1024,512]{1,0:T(8,128)(2,1)}, f32[2,2,512]{2,1,0:T(2,128)}, bf16[2,512,512]{2,1,0:T(8,128)(2,1)}) custom-call(s32[8,8]{1,0:T(8,128)} %src_ref.1, s32[1,64]{1,0:T(1,128)} %sel_row_ref.1, f32[2,2,512]{2,1,0:T(2,128)} %master_ref.1, f32[2,2,512]{2,1,0:T(2,128)} %first_ref.1, ...), custom_call_target="tpu_custom_call" | custom-call | flops 12884901888 | bytes 12582912 | tf_op jit(solution)/shard_map/pallas_call | solution.py:521
  113.9 0.0 copy-start.2
  114.0 0.0 copy-start.1
  114.0 2.4 %copy.20 = bf16[1024,512]{1,0:T(8,128)(2,1)} copy(bf16[1024,512]{1,0:T(8,128)(2,1)} %get-tuple-element.10) | data formatting | bytes 2097152
  116.4 0.0 copy-done.2
  116.4 0.0 copy-start.3
  116.4 0.0 copy-start
  116.4 1.0 copy.21
  117.4 0.0 copy-done.1
  117.4 1.0 copy.22
  118.3 0.0 copy-done.3
  118.3 0.6 copy.23
  118.9 0.0 copy-done
  118.9 1.0 copy.24
Async XLA Ops:
  113.9 2.4 %copy-start.2 = (bf16[1024,512]{1,0:T(8,128)(2,1)S(1)}, bf16[1024,512]{1,0:T(8,128)(2,1)}, u32[]{:S(2)}) copy-start(bf16[1024,512]{1,0:T(8,128)(2,1)} %get-tuple-element.11) | copy-start | bytes 3145732
  114.0 3.4 %copy-start.1 = (bf16[1024,512]{1,0:T(8,128)(2,1)S(1)}, bf16[1024,512]{1,0:T(8,128)(2,1)}, u32[]{:S(2)}) copy-start(bf16[1024,512]{1,0:T(8,128)(2,1)} %get-tuple-element.12) | copy-start | bytes 3145732
  116.4 1.9 %copy-start.3 = (f32[2,2,512]{2,1,0:T(2,128)S(1)}, f32[2,2,512]{2,1,0:T(2,128)}, u32[]{:S(2)}) copy-start(f32[2,2,512]{2,1,0:T(2,128)} %get-tuple-element.13) | copy-start | bytes 24580
  116.4 2.5 %copy-start = (bf16[2,512,512]{2,1,0:T(8,128)(2,1)S(1)}, bf16[2,512,512]{2,1,0:T(8,128)(2,1)}, u32[]{:S(2)}) copy-start(bf16[2,512,512]{2,1,0:T(8,128)(2,1)} %get-tuple-element.14) | copy-start | bytes 3145732

commit v2 on v1

--- a/solution.py
+++ b/solution.py
@@ -70,6 +70,7 @@
     rim,
     tiles,
     dense,
+    dense_low,
     out_grad,
     stale_features,
     stale_grads,
@@ -304,7 +305,9 @@
                 ids = src_wide[rows_of(i, 8), t * 128 : (t + 1) * 128]
                 chosen = (ids == target).astype(F32)[0:1, :]
                 total = total + tiles[i, t].astype(F32) * chosen
-            dense[rows_of(i, 128), rows_of(b, 128)] = total.astype(BF16)
+            high = total.astype(BF16)
+            dense[rows_of(i, 128), rows_of(b, 128)] = high
+            dense_low[rows_of(i, 128), rows_of(b, 128)] = (total - high.astype(F32)).astype(BF16)
 
         repeat(16, column)
 
@@ -317,6 +320,14 @@
     loads[2].wait()
     gather_end(0, gather_now, weights)
 
+    def tiles_on(rows, columns, table):
+        return dot(dense[rows, columns], table) + dot(dense_low[rows, columns], table)
+
+    def tiles_back(columns):
+        return dot_over_rows(dense[:, columns], upstream[...]) + dot_over_rows(
+            dense_low[:, columns], upstream[...]
+        )
+
     def up(i):
         rows = rows_of(i, 256)
         upstream[rows, :] = dot_over_columns(out_grad[rows, :], weights[1]).astype(BF16)
@@ -324,7 +335,7 @@
     repeat(4, up)
 
     def rim_part(i):
-        part = dot_over_rows(dense[:, rows_of(i + 4, 256)], upstream[...])
+        part = tiles_back(rows_of(i + 4, 256))
         grad_send[rows_of(i, 256), :] = part.astype(BF16)
 
     repeat(4, rim_part)
@@ -340,16 +351,14 @@
         rows = rows_of(i, 256)
         row = lax.broadcasted_iota(jnp.int32, (256, NODES), 0) + i * 256
         placing = (row == wanted).astype(F32).astype(BF16)
-        d_first[rows, :] = dot_over_rows(dense[:, rows], upstream[...]) + dot(
-            placing, stale_grads[...]
-        )
+        d_first[rows, :] = tiles_back(rows) + dot(placing, stale_grads[...])
 
     repeat(4, local_part)
 
     def ahead(i):
         rows = rows_of(i, 256)
-        p_local[rows, :] = dot(dense[rows, 0:NODES], features[...])
-        p_stale[rows, :] = dot(dense[rows, NODES : 2 * NODES], stale_features[...])
+        p_local[rows, :] = tiles_on(rows, slice(0, NODES), features[...])
+        p_stale[rows, :] = tiles_on(rows, slice(NODES, 2 * NODES), stale_features[...])
 
     repeat(4, ahead)
 
@@ -357,7 +366,7 @@
 
     def first_layer(i):
         rows = rows_of(i, 256)
-        p = (p_local[rows, :] + dot(dense[rows, NODES : 2 * NODES], rim[...])).astype(BF16)
+        p = (p_local[rows, :] + tiles_on(rows, slice(NODES, 2 * NODES), rim[...])).astype(BF16)
         p_first[rows, :] = p
         zf = dot(p, weights[0])
         s = 1.0 / (1.0 + jnp.exp(-zf))
@@ -376,7 +385,7 @@
 
     def second_layer(i):
         rows = rows_of(i, 256)
-        p_second[rows, :] = (p_stale[rows, :] + dot(dense[rows, 0:NODES], hidden[...])).astype(BF16)
+        p_second[rows, :] = (p_stale[rows, :] + tiles_on(rows, slice(0, NODES), hidden[...])).astype(BF16)
 
     repeat(4, second_layer)
 
@@ -533,6 +542,7 @@
             nodes,
             nodes,
             pltpu.VMEM((8, 8, 128, 128), BF16),
+            pltpu.VMEM((NODES, 2 * NODES), BF16),
             pltpu.VMEM((NODES, 2 * NODES), BF16),
             nodes,
             nodes,

time: 120 us -> 120 us (level)
  no operation moved by 1% of the time
where the time goes in v2:
time: 120 us
  Pallas kernels  113 us (94%)
  local copies, waits for them, and re-layouts  5.93 us (5%)
    pallas_call x1, Pallas kernels, per_device(): pl.pallas_call(kernel, out_shape=(rows, rows, rows, jax.ShapeDtypeStruct(...  113 us
    unnamed x13, local copies, waits for them, and re-layouts  5.93 us

profile of v2, /device:TPU:1, one launch (start us, length us, event | category | flops | bytes accessed | tf_op | source)
XLA Modules:
  0.0 119.8 jit_solution(18071311198223650900)
XLA Ops:
  0.6 113.2 %shard_map.137 = (bf16[1024,512]{1,0:T(8,128)(2,1)}, bf16[1024,512]{1,0:T(8,128)(2,1)}, bf16[1024,512]{1,0:T(8,128)(2,1)}, f32[2,2,512]{2,1,0:T(2,128)}, bf16[2,512,512]{2,1,0:T(8,128)(2,1)}) custom-call(s32[8,8]{1,0:T(8,128)} %src_ref.1, s32[1,64]{1,0:T(1,128)} %sel_row_ref.1, f32[2,2,512]{2,1,0:T(2,128)} %master_ref.1, f32[2,2,512]{2,1,0:T(2,128)} %first_ref.1, ...), custom_call_target="tpu_custom_call" | custom-call | flops 12884901888 | bytes 12582912 | tf_op jit(solution)/shard_map/pallas_call | solution.py:530
  113.8 0.0 copy-start.2
  113.8 0.0 copy-start.1
  113.8 2.4 %copy.20 = bf16[1024,512]{1,0:T(8,128)(2,1)} copy(bf16[1024,512]{1,0:T(8,128)(2,1)} %get-tuple-element.10) | data formatting | bytes 2097152
  116.2 0.0 copy-done.2
  116.2 0.0 copy-start.3
  116.2 0.0 copy-start
  116.2 1.0 copy.21
  117.2 0.0 copy-done.1
  117.2 1.0 copy.22
  118.2 0.0 copy-done.3
  118.2 0.6 copy.23
  118.8 0.0 copy-done
  118.8 1.0 copy.24
Async XLA Ops:
  113.8 2.4 %copy-start.2 = (bf16[1024,512]{1,0:T(8,128)(2,1)S(1)}, bf16[1024,512]{1,0:T(8,128)(2,1)}, u32[]{:S(2)}) copy-start(bf16[1024,512]{1,0:T(8,128)(2,1)} %get-tuple-element.11) | copy-start | bytes 3145732
  113.8 3.4 %copy-start.1 = (bf16[1024,512]{1,0:T(8,128)(2,1)S(1)}, bf16[1024,512]{1,0:T(8,128)(2,1)}, u32[]{:S(2)}) copy-start(bf16[1024,512]{1,0:T(8,128)(2,1)} %get-tuple-element.12) | copy-start | bytes 3145732
  116.2 1.9 %copy-start.3 = (f32[2,2,512]{2,1,0:T(2,128)S(1)}, f32[2,2,512]{2,1,0:T(2,128)}, u32[]{:S(2)}) copy-start(f32[2,2,512]{2,1,0:T(2,128)} %get-tuple-element.13) | copy-start | bytes 24580
  116.2 2.5 %copy-start = (bf16[2,512,512]{2,1,0:T(8,128)(2,1)S(1)}, bf16[2,512,512]{2,1,0:T(8,128)(2,1)}, u32[]{:S(2)}) copy-start(bf16[2,512,512]{2,1,0:T(8,128)(2,1)} %get-tuple-element.14) | copy-start | bytes 3145732

commit v3 on v2

--- a/solution.py
+++ b/solution.py
@@ -93,9 +93,9 @@
     grad_blocks,
     from_core,
     core_sum,
-    from_y,
-    y_sum,
-    from_plane,
+    from_across,
+    across_sum,
+    from_z,
     shard_now,
     shard_next,
     rows_f32,
@@ -110,8 +110,8 @@
     recv_sem,
 ):
     z, x, c, y = (lax.axis_index(a) for a in DEVICES)
-    plane = z * NX + x
-    me = plane * NC + c
+    column = x * NY + y
+    me = (z * NX + x) * NC + c
 
     loads = [
         pltpu.make_async_copy(s, d, load_sem.at[i])
@@ -129,11 +129,13 @@
         load.start()
 
     def peer_at(step):
-        dz_, dx_, dc_ = step // 8, (step // 2) % 4, step % 2
+        turn, dx_, dc_ = step % 8, (step // 8) % 4, step // 32
+        half = (turn + 1) // 2
+        dz_ = half * (turn % 2) + (NZ - half) * (1 - turn % 2)
         return ((z + dz_) % NZ, (x + dx_) % NX, (c + dc_) % NC)
 
-    def plane_at(step):
-        return ((z + step // 4) % NZ, (x + step % 4) % NX)
+    def across(step):
+        return ((x + step // NY) % NX, (y + step % NY) % NY)
 
     barrier = pltpu.get_barrier_semaphore()
 
@@ -142,10 +144,10 @@
         pl.semaphore_signal(barrier, inc=1, device_id=(pz, px, pc, y), device_id_type=MESH)
 
     repeat(PEERS - 1, greet)
-    for k in range(1, NY):
-        pl.semaphore_signal(
-            barrier, inc=1, device_id=(z, x, c, (y + k) % NY), device_id_type=MESH
-        )
+    for step in range(1, NX * NY):
+        if step % NY:
+            px, py = across(step)
+            pl.semaphore_signal(barrier, inc=1, device_id=(z, px, c, py), device_id_type=MESH)
 
     def fill_rows(target, source):
         for m in range(2):
@@ -161,7 +163,7 @@
 
     def bits(o):
         m, j, p = o >> 7, (o >> 5) & 3, (o >> 4) & 1
-        return (((o >> 3) & 1) << 7) | (((o >> 1) & 3) << 5) | (p << 4) | (m << 3) | ((o & 1) << 2) | j
+        return (((o >> 3) & 1) << 7) | (p << 6) | (((o >> 1) & 3) << 4) | (m << 3) | ((o & 1) << 2) | j
 
     down = lax.broadcasted_iota(jnp.int32, (256, 256), 0)
     along = lax.broadcasted_iota(jnp.int32, (256, 256), 1)
@@ -190,25 +192,21 @@
 
     repeat(4, choose_rows)
 
-    pl.semaphore_wait(barrier, PEERS - 1 + NY - 1)
+    pl.semaphore_wait(barrier, PEERS - 1 + NX * (NY - 1))
 
     def spread_shard(slot, shard, gathered):
-        gathered[c, y, rows_of(plane, 16), :] = shard[...]
-
-        def send(i):
-            pz, px = plane_at(i + 1)
+        gathered[c, column, rows_of(z, 16), :] = shard[...]
+        for k in range(1, NZ):
             pltpu.make_async_remote_copy(
                 src_ref=shard,
-                dst_ref=gathered.at[c, y, rows_of(plane, 16)],
+                dst_ref=gathered.at[c, column, rows_of(z, 16)],
                 send_sem=send_sem.at[slot],
                 recv_sem=recv_sem.at[slot],
-                device_id=(pz, px, c, y),
+                device_id=((z + k) % NZ, x, c, y),
                 device_id_type=MESH,
             ).start()
 
-        repeat(NZ * NX - 1, send)
-
-    def plane_bytes(slot, ref):
+    def total_of(slot, ref):
         return pltpu.make_async_remote_copy(
             src_ref=ref,
             dst_ref=ref,
@@ -218,24 +216,21 @@
             device_id_type=MESH,
         )
 
-    def gather_y(slot, gathered):
-        plane_bytes(slot, gathered.at[0, 0, pl.ds(0, 496)]).wait_recv()
-        copies = [
+    def gather_across(slot, gathered):
+        total_of(slot, gathered.at[0, 0, pl.ds(0, 112)]).wait_recv()
+        for step in range(1, NX * NY):
+            px, py = across(step)
             pltpu.make_async_remote_copy(
-                src_ref=gathered.at[c, y],
-                dst_ref=gathered.at[c, y],
+                src_ref=gathered.at[c, column],
+                dst_ref=gathered.at[c, column],
                 send_sem=send_sem.at[slot + 1],
                 recv_sem=recv_sem.at[slot + 1],
-                device_id=(z, x, c, (y + k) % NY),
+                device_id=(z, px, c, py),
                 device_id_type=MESH,
-            )
-            for k in range(1, NY)
-        ]
-        for copy in copies:
-            copy.start()
+            ).start()
 
     def gather_core(slot, gathered):
-        plane_bytes(slot + 1, gathered.at[0, pl.ds(0, 3)]).wait_recv()
+        total_of(slot + 1, gathered.at[0, pl.ds(0, 15)]).wait_recv()
         pltpu.make_async_remote_copy(
             src_ref=gathered.at[c],
             dst_ref=gathered.at[c],
@@ -246,11 +241,12 @@
         ).start()
 
     def gather_end(slot, gathered, whole):
-        plane_bytes(slot + 2, gathered.at[0]).wait_recv()
+        total_of(slot + 2, gathered.at[0]).wait_recv()
 
         def lay(chunk):
+            at_z, pair = rows_of(chunk // 2, 16), (chunk % 2) * 8
             taken = jnp.concatenate(
-                [gathered[a // 4, a % 4, rows_of(chunk, 32), :] for a in range(8)], 0
+                [gathered[a // 8, pair + a % 8, at_z, :] for a in range(16)], 0
             )
             laid = dot(perm[...], taken).astype(BF16)
             for m in range(2):
@@ -267,9 +263,9 @@
 
         repeat(4, pick)
 
-    def send_pieces(slot, source, target):
+    def send_pieces(slot, source, target, begin, end):
         def send(i):
-            pz, px, pc = peer_at(i + 1)
+            pz, px, pc = peer_at(i + begin)
             peer = (pz * NX + px) * NC + pc
             pltpu.make_async_remote_copy(
                 src_ref=source.at[rows_of(peer, PIECE)],
@@ -280,14 +276,14 @@
                 device_id_type=MESH,
             ).start()
 
-        repeat(PEERS - 1, send)
+        repeat(end - begin, send)
 
     sent_bytes = pl.ds(0, (PEERS - 1) * PIECE)
 
     spread_shard(0, shard_now, gather_now)
     loads[0].wait()
     pick_pieces(raw_send, features)
-    send_pieces(3, raw_send, rim)
+    send_pieces(3, raw_send, rim, 1, 16)
     rim[rows_of(me, PIECE), :] = raw_send[rows_of(me, PIECE), :]
 
     tile_of = lax.broadcasted_iota(jnp.int32, (8, 1024), 1) // 128
@@ -311,11 +307,13 @@
 
         repeat(16, column)
 
-    repeat(3, densify)
-    gather_y(0, gather_now)
-    repeat(3, lambda i: densify(i + 3))
+    repeat(1, densify)
+    gather_across(0, gather_now)
+    send_pieces(3, raw_send, rim, 16, 40)
+    repeat(3, lambda i: densify(i + 1))
     gather_core(0, gather_now)
-    repeat(2, lambda i: densify(i + 6))
+    send_pieces(3, raw_send, rim, 40, 64)
+    repeat(4, lambda i: densify(i + 4))
 
     loads[2].wait()
     gather_end(0, gather_now, weights)
@@ -339,7 +337,7 @@
         grad_send[rows_of(i, 256), :] = part.astype(BF16)
 
     repeat(4, rim_part)
-    send_pieces(4, grad_send, fresh_grads_hbm)
+    send_pieces(4, grad_send, fresh_grads_hbm, 1, 32)
     own_grads = pltpu.make_async_copy(
         grad_send.at[rows_of(me, PIECE)], fresh_grads_hbm.at[rows_of(me, PIECE)], store_sem.at[0]
     )
@@ -362,7 +360,7 @@
 
     repeat(4, ahead)
 
-    plane_bytes(3, rim.at[sent_bytes]).wait_recv()
+    total_of(3, rim.at[sent_bytes]).wait_recv()
 
     def first_layer(i):
         rows = rows_of(i, 256)
@@ -375,7 +373,6 @@
 
     repeat(4, first_layer)
     pick_pieces(feature_send, hidden)
-    send_pieces(5, feature_send, fresh_features_hbm)
     own_features = pltpu.make_async_copy(
         feature_send.at[rows_of(me, PIECE)],
         fresh_features_hbm.at[rows_of(me, PIECE)],
@@ -403,10 +400,9 @@
                 0,
             )
             blocks = dot(perm_back[...], stacked).astype(BF16)
-            for a in range(8):
-                grad_blocks[a // 4, a % 4, rows_of(i * chunk + k, 32), :] = blocks[
-                    a * 32 : (a + 1) * 32
-                ]
+            at_z, pair = rows_of(i * 4 + k // 2, 16), (k % 2) * 8
+            for a in range(16):
+                grad_blocks[a // 8, pair + a % 8, at_z, :] = blocks[a * 16 : (a + 1) * 16]
 
     repeat(2, grad_rows)
 
@@ -419,6 +415,8 @@
         device_id_type=MESH,
     ).start()
 
+    send_pieces(4, grad_send, fresh_grads_hbm, 32, 48)
+
     def last(i):
         rows = rows_of(i, 256)
         layer_out[rows, :] = dot(p_second[rows, :], weights[1]).astype(BF16)
@@ -427,43 +425,44 @@
     store_layer = pltpu.make_async_copy(layer_out, layer_out_hbm, store_sem.at[2])
     store_layer.start()
 
-    plane_bytes(6, from_core).wait_recv()
-    for k in range(NY):
+    total_of(6, from_core).wait_recv()
+
+    def add_core(k):
         core_sum[k] = (grad_blocks[c, k].astype(F32) + from_core[k].astype(F32)).astype(BF16)
-    for k in range(1, NY):
+
+    repeat(NX * NY, add_core)
+    for step in range(1, NX * NY):
+        px, py = across(step)
         pltpu.make_async_remote_copy(
-            src_ref=core_sum.at[(y + k) % NY],
-            dst_ref=from_y.at[k - 1],
+            src_ref=core_sum.at[px * NY + py],
+            dst_ref=from_across.at[step - 1],
             send_sem=send_sem.at[7],
             recv_sem=recv_sem.at[7],
-            device_id=(z, x, c, (y + k) % NY),
+            device_id=(z, px, c, py),
             device_id_type=MESH,
         ).start()
-    plane_bytes(7, from_y).wait_recv()
-    y_sum[...] = (
-        core_sum[y].astype(F32)
-        + from_y[0].astype(F32)
-        + from_y[1].astype(F32)
-        + from_y[2].astype(F32)
-    ).astype(BF16)
-    from_plane[rows_of(plane, 16), :] = y_sum[rows_of(plane, 16), :]
-
-    def send_shard(i):
-        pz, px = plane_at(i + 1)
+    send_pieces(4, grad_send, fresh_grads_hbm, 48, 64)
+    total_of(7, from_across).wait_recv()
+    across_total = core_sum[column].astype(F32)
+    for k in range(NX * NY - 1):
+        across_total = across_total + from_across[k].astype(F32)
+    across_sum[...] = across_total.astype(BF16)
+    from_z[rows_of(z, 16), :] = across_sum[rows_of(z, 16), :]
+    for k in range(1, NZ):
+        pz = (z + k) % NZ
         pltpu.make_async_remote_copy(
-            src_ref=y_sum.at[rows_of(pz * NX + px, 16)],
-            dst_ref=from_plane.at[rows_of(plane, 16)],
+            src_ref=across_sum.at[rows_of(pz, 16)],
+            dst_ref=from_z.at[rows_of(z, 16)],
             send_sem=send_sem.at[8],
             recv_sem=recv_sem.at[8],
-            device_id=(pz, px, c, y),
+            device_id=(pz, x, c, y),
             device_id_type=MESH,
         ).start()
-
-    repeat(NZ * NX - 1, send_shard)
-    plane_bytes(8, from_plane.at[pl.ds(0, 496)]).wait_recv()
-    total = from_plane[0:16, :].astype(F32)
-    for k in range(1, NZ * NX):
-        total = total + from_plane[k * 16 : (k + 1) * 16, :].astype(F32)
+    send_pieces(5, feature_send, fresh_features_hbm, 1, 16)
+    total_of(8, from_z.at[pl.ds(0, 112)]).wait_recv()
+    total = from_z[0:16, :].astype(F32)
+    for k in range(1, NZ):
+        total = total + from_z[k * 16 : (k + 1) * 16, :].astype(F32)
     grads = total / TOTAL_NODES
     moment_new = decay_first * rows_f32[1] + (1.0 - decay_first) * grads
     second_new = decay_second * rows_f32[2] + (1.0 - decay_second) * grads * grads
@@ -476,32 +475,46 @@
     rows_f32[3] = master_next
     shard_next[...] = master_next.astype(BF16)
     spread_shard(9, shard_next, gather_next)
+    send_pieces(5, feature_send, fresh_features_hbm, 16, 28)
     for m in range(2):
         for r in range(2):
             for j in range(4):
                 s = m * 8 + r * 4 + j
                 master_next_ref[m, r : r + 1, j * 128 : (j + 1) * 128] = rows_f32[3, s : s + 1, :]
-    gather_y(9, gather_next)
+    gather_across(9, gather_next)
+    send_pieces(5, feature_send, fresh_features_hbm, 28, 44)
     gather_core(9, gather_next)
+    send_pieces(5, feature_send, fresh_features_hbm, 44, 64)
     gather_end(9, gather_next, weights_next)
     store_weights = pltpu.make_async_copy(weights_next, weights_next_hbm, store_sem.at[3])
     store_weights.start()
 
-    for slot, shard, gathered in ((0, gather_now, gather_now), (9, gather_next, gather_next)):
-        plane_bytes(slot, gathered.at[0, 0, pl.ds(0, 496)]).wait_send()
-        plane_bytes(slot + 1, gathered.at[0, pl.ds(0, 3)]).wait_send()
-        plane_bytes(slot + 2, gathered.at[0]).wait_send()
-    plane_bytes(6, from_core).wait_send()
-    plane_bytes(7, from_y).wait_send()
-    plane_bytes(8, from_plane.at[pl.ds(0, 496)]).wait_send()
+    for slot, gathered in ((0, gather_now), (9, gather_next)):
+        total_of(slot, gathered.at[0, 0, pl.ds(0, 112)]).wait_send()
+        total_of(slot + 1, gathered.at[0, pl.ds(0, 15)]).wait_send()
+        total_of(slot + 2, gathered.at[0]).wait_send()
+    total_of(6, from_core).wait_send()
+    total_of(7, from_across).wait_send()
+    total_of(8, from_z.at[pl.ds(0, 112)]).wait_send()
     for slot, source in ((3, raw_send), (4, grad_send), (5, feature_send)):
-        plane_bytes(slot, source.at[sent_bytes]).wait_send()
-    plane_bytes(4, fresh_grads_hbm.at[sent_bytes]).wait_recv()
-    plane_bytes(5, fresh_features_hbm.at[sent_bytes]).wait_recv()
+        total_of(slot, source.at[sent_bytes]).wait_send()
+    total_of(4, fresh_grads_hbm.at[sent_bytes]).wait_recv()
+    total_of(5, fresh_features_hbm.at[sent_bytes]).wait_recv()
     own_grads.wait()
     own_features.wait()
     store_layer.wait()
     store_weights.wait()
+
+
+def deliver(*refs):
+    sources, targets, sem = refs[:5], refs[5:10], refs[10]
+    copies = [
+        pltpu.make_async_copy(s, t, sem.at[i]) for i, (s, t) in enumerate(zip(sources, targets))
+    ]
+    for copy in copies:
+        copy.start()
+    for copy in copies:
+        copy.wait()
 
 
 def per_device(
@@ -521,21 +534,22 @@
     nodes = pltpu.VMEM((NODES, F), BF16)
     nodes_f32 = pltpu.VMEM((NODES, F), F32)
     matrices = pltpu.VMEM((2, F, F), BF16)
-    blocks = pltpu.VMEM((2, NY, 512, 128), BF16)
-    half = pltpu.VMEM((NY, 512, 128), BF16)
-    lines = pltpu.VMEM((512, 128), BF16)
+    blocks = pltpu.VMEM((2, NX * NY, 128, 128), BF16)
+    half = pltpu.VMEM((NX * NY, 128, 128), BF16)
+    lines = pltpu.VMEM((128, 128), BF16)
     shard = pltpu.VMEM((16, 128), BF16)
     square = pltpu.VMEM((256, 256), BF16)
     rows = jax.ShapeDtypeStruct((NODES, F), BF16)
-    return pl.pallas_call(
+    shapes = (
+        rows,
+        rows,
+        rows,
+        jax.ShapeDtypeStruct((2, 2, F), F32),
+        jax.ShapeDtypeStruct((2, F, F), BF16),
+    )
+    made = pl.pallas_call(
         kernel,
-        out_shape=(
-            rows,
-            rows,
-            rows,
-            jax.ShapeDtypeStruct((2, 2, F), F32),
-            jax.ShapeDtypeStruct((2, F, F), BF16),
-        ),
+        out_shape=shapes,
         in_specs=[vmem, vmem, vmem, vmem, vmem] + [any_space] * 5,
         out_specs=(any_space, any_space, any_space, vmem, any_space),
         scratch_shapes=[
@@ -566,7 +580,7 @@
             blocks,
             half,
             half,
-            pltpu.VMEM((NY - 1, 512, 128), BF16),
+            pltpu.VMEM((NX * NY - 1, 128, 128), BF16),
             lines,
             lines,
             shard,
@@ -600,6 +614,13 @@
         stale_grads,
         out_grad,
     )
+    return pl.pallas_call(
+        deliver,
+        out_shape=shapes,
+        in_specs=[any_space] * 5,
+        out_specs=(any_space,) * 5,
+        scratch_shapes=[pltpu.SemaphoreType.DMA((5,))],
+    )(*made)
 
 
 def solution(mesh):

time: 120 us -> 244 us (2.03)
  Pallas kernels: 113 us -> 243 us
  local copies, waits for them, and re-layouts: 5.93 us -> 0 us
    pallas_call x1 -> x2, Pallas kernels: 113 us -> 243 us  [the longest x1 128 us: per_device(): pl.pallas_call(deliver, out_shape=shapes, in_specs=[any_space] * 5, out_s...]
    unnamed x13 -> x0, local copies, waits for them, and re-layouts: 5.93 us -> none
where the time goes in v3:
time: 244 us; the launch traced here: 243 us
  Pallas kernels  243 us (100%)
    pallas_call x1, Pallas kernels, per_device(): pl.pallas_call(deliver, out_shape=shapes, in_specs=[any_space] * 5, out_s...  128 us
    pallas_call x1, Pallas kernels, per_device(): pl.pallas_call(kernel, out_shape=shapes, in_specs=[vmem, vmem, vmem, vmem...  114 us

profile of v3, /device:TPU:1, one launch (start us, length us, event | category | flops | bytes accessed | tf_op | source)
XLA Modules:
  0.0 243.4 jit_solution(18279410616949986783)
XLA Ops:
  0.6 114.3 %shard_map.137 = (bf16[1024,512]{1,0:T(8,128)(2,1)}, bf16[1024,512]{1,0:T(8,128)(2,1)}, bf16[1024,512]{1,0:T(8,128)(2,1)}, f32[2,2,512]{2,1,0:T(2,128)}, bf16[2,512,512]{2,1,0:T(8,128)(2,1)}) custom-call(s32[8,8]{1,0:T(8,128)} %src_ref.1, s32[1,64]{1,0:T(1,128)} %sel_row_ref.1, f32[2,2,512]{2,1,0:T(2,128)} %master_ref.1, f32[2,2,512]{2,1,0:T(2,128)} %first_ref.1, ...), custom_call_target="tpu_custom_call" | custom-call | flops 12884901888 | bytes 12582912 | tf_op jit(solution)/shard_map/pallas_call | solution.py:550
  114.9 128.5 %shard_map.138 = (bf16[1024,512]{1,0:T(8,128)(2,1)}, bf16[1024,512]{1,0:T(8,128)(2,1)}, bf16[1024,512]{1,0:T(8,128)(2,1)}, f32[2,2,512]{2,1,0:T(2,128)}, bf16[2,512,512]{2,1,0:T(8,128)(2,1)}) custom-call(bf16[1024,512]{1,0:T(8,128)(2,1)} %get-tuple-element.10.refs_0_, bf16[1024,512]{1,0:T(8,128)(2,1)} %get-tuple-element.11.refs_1_, ...), custom_call_target="tpu_custom_call" | custom-call | tf_op jit(solution)/shard_map/pallas_call | solution.py:617

commit v4 on v3

--- a/solution.py
+++ b/solution.py
@@ -243,18 +243,31 @@
     def gather_end(slot, gathered, whole):
         total_of(slot + 2, gathered.at[0]).wait_recv()
 
-        def lay(chunk):
-            at_z, pair = rows_of(chunk // 2, 16), (chunk % 2) * 8
+        def lay(group):
             taken = jnp.concatenate(
-                [gathered[a // 8, pair + a % 8, at_z, :] for a in range(16)], 0
+                [
+                    jnp.concatenate(
+                        [
+                            gathered[a // 8, (k % 2) * 8 + a % 8, rows_of(group * 2 + k // 2, 16), :]
+                            for a in range(16)
+                        ],
+                        0,
+                    )
+                    for k in range(4)
+                ],
+                1,
             )
             laid = dot(perm[...], taken).astype(BF16)
-            for m in range(2):
-                for j in range(4):
-                    at = (m * 4 + j) * 32
-                    whole[m, rows_of(chunk, 32), j * 128 : (j + 1) * 128] = laid[at : at + 32]
-
-        repeat(16, lay)
+            for k in range(4):
+                rows = rows_of(group * 4 + k, 32)
+                for m in range(2):
+                    for j in range(4):
+                        at = (m * 4 + j) * 32
+                        whole[m, rows, j * 128 : (j + 1) * 128] = laid[
+                            at : at + 32, k * 128 : (k + 1) * 128
+                        ]
+
+        repeat(4, lay)
 
     def pick_pieces(target, table):
         def pick(i):
@@ -283,7 +296,6 @@
     spread_shard(0, shard_now, gather_now)
     loads[0].wait()
     pick_pieces(raw_send, features)
-    send_pieces(3, raw_send, rim, 1, 16)
     rim[rows_of(me, PIECE), :] = raw_send[rows_of(me, PIECE), :]
 
     tile_of = lax.broadcasted_iota(jnp.int32, (8, 1024), 1) // 128
@@ -309,56 +321,56 @@
 
     repeat(1, densify)
     gather_across(0, gather_now)
-    send_pieces(3, raw_send, rim, 16, 40)
+    send_pieces(3, raw_send, rim, 1, 32)
     repeat(3, lambda i: densify(i + 1))
     gather_core(0, gather_now)
-    send_pieces(3, raw_send, rim, 40, 64)
+    send_pieces(3, raw_send, rim, 32, 64)
     repeat(4, lambda i: densify(i + 4))
 
     loads[2].wait()
-    gather_end(0, gather_now, weights)
+    loads[4].wait()
 
     def tiles_on(rows, columns, table):
         return dot(dense[rows, columns], table) + dot(dense_low[rows, columns], table)
 
+    def ahead(i):
+        rows = rows_of(i, 256)
+        p_local[rows, :] = tiles_on(rows, slice(0, NODES), features[...])
+        p_stale[rows, :] = tiles_on(rows, slice(NODES, 2 * NODES), stale_features[...])
+
+    repeat(4, ahead)
+
+    gather_end(0, gather_now, weights)
+
     def tiles_back(columns):
-        return dot_over_rows(dense[:, columns], upstream[...]) + dot_over_rows(
-            dense_low[:, columns], upstream[...]
-        )
+        return dot(upstream[...], dense[:, columns]) + dot(upstream[...], dense_low[:, columns])
 
     def up(i):
         rows = rows_of(i, 256)
-        upstream[rows, :] = dot_over_columns(out_grad[rows, :], weights[1]).astype(BF16)
+        upstream[:, rows] = dot_over_columns(weights[1], out_grad[rows, :]).astype(BF16)
 
     repeat(4, up)
 
     def rim_part(i):
         part = tiles_back(rows_of(i + 4, 256))
-        grad_send[rows_of(i, 256), :] = part.astype(BF16)
+        grad_send[rows_of(i, 256), :] = part.astype(BF16).T
 
     repeat(4, rim_part)
-    send_pieces(4, grad_send, fresh_grads_hbm, 1, 32)
+    send_pieces(4, grad_send, fresh_grads_hbm, 1, 48)
     own_grads = pltpu.make_async_copy(
         grad_send.at[rows_of(me, PIECE)], fresh_grads_hbm.at[rows_of(me, PIECE)], store_sem.at[0]
     )
     own_grads.start()
 
     loads[3].wait()
-    loads[4].wait()
     def local_part(i):
         rows = rows_of(i, 256)
         row = lax.broadcasted_iota(jnp.int32, (256, NODES), 0) + i * 256
         placing = (row == wanted).astype(F32).astype(BF16)
-        d_first[rows, :] = tiles_back(rows) + dot(placing, stale_grads[...])
+        d_first[rows, :] = tiles_back(rows).T + dot(placing, stale_grads[...])
 
     repeat(4, local_part)
 
-    def ahead(i):
-        rows = rows_of(i, 256)
-        p_local[rows, :] = tiles_on(rows, slice(0, NODES), features[...])
-        p_stale[rows, :] = tiles_on(rows, slice(NODES, 2 * NODES), stale_features[...])
-
-    repeat(4, ahead)
 
     total_of(3, rim.at[sent_bytes]).wait_recv()
 
@@ -373,6 +385,7 @@
 
     repeat(4, first_layer)
     pick_pieces(feature_send, hidden)
+    send_pieces(4, grad_send, fresh_grads_hbm, 48, 64)
     own_features = pltpu.make_async_copy(
         feature_send.at[rows_of(me, PIECE)],
         fresh_features_hbm.at[rows_of(me, PIECE)],
@@ -415,7 +428,6 @@
         device_id_type=MESH,
     ).start()
 
-    send_pieces(4, grad_send, fresh_grads_hbm, 32, 48)
 
     def last(i):
         rows = rows_of(i, 256)
@@ -427,10 +439,11 @@
 
     total_of(6, from_core).wait_recv()
 
-    def add_core(k):
-        core_sum[k] = (grad_blocks[c, k].astype(F32) + from_core[k].astype(F32)).astype(BF16)
-
-    repeat(NX * NY, add_core)
+    def add_core(i):
+        four = pl.ds(i * 4, 4)
+        core_sum[four] = (grad_blocks[c, four].astype(F32) + from_core[four].astype(F32)).astype(BF16)
+
+    repeat(4, add_core)
     for step in range(1, NX * NY):
         px, py = across(step)
         pltpu.make_async_remote_copy(
@@ -441,7 +454,7 @@
             device_id=(z, px, c, py),
             device_id_type=MESH,
         ).start()
-    send_pieces(4, grad_send, fresh_grads_hbm, 48, 64)
+    send_pieces(5, feature_send, fresh_features_hbm, 1, 12)
     total_of(7, from_across).wait_recv()
     across_total = core_sum[column].astype(F32)
     for k in range(NX * NY - 1):
@@ -458,7 +471,7 @@
             device_id=(pz, x, c, y),
             device_id_type=MESH,
         ).start()
-    send_pieces(5, feature_send, fresh_features_hbm, 1, 16)
+    send_pieces(5, feature_send, fresh_features_hbm, 12, 24)
     total_of(8, from_z.at[pl.ds(0, 112)]).wait_recv()
     total = from_z[0:16, :].astype(F32)
     for k in range(1, NZ):
@@ -475,16 +488,16 @@
     rows_f32[3] = master_next
     shard_next[...] = master_next.astype(BF16)
     spread_shard(9, shard_next, gather_next)
-    send_pieces(5, feature_send, fresh_features_hbm, 16, 28)
+    send_pieces(5, feature_send, fresh_features_hbm, 24, 34)
     for m in range(2):
         for r in range(2):
             for j in range(4):
                 s = m * 8 + r * 4 + j
                 master_next_ref[m, r : r + 1, j * 128 : (j + 1) * 128] = rows_f32[3, s : s + 1, :]
     gather_across(9, gather_next)
-    send_pieces(5, feature_send, fresh_features_hbm, 28, 44)
+    send_pieces(5, feature_send, fresh_features_hbm, 34, 50)
     gather_core(9, gather_next)
-    send_pieces(5, feature_send, fresh_features_hbm, 44, 64)
+    send_pieces(5, feature_send, fresh_features_hbm, 50, 64)
     gather_end(9, gather_next, weights_next)
     store_weights = pltpu.make_async_copy(weights_next, weights_next_hbm, store_sem.at[3])
     store_weights.start()
@@ -507,13 +520,22 @@
 
 
 def deliver(*refs):
-    sources, targets, sem = refs[:5], refs[5:10], refs[10]
-    copies = [
-        pltpu.make_async_copy(s, t, sem.at[i]) for i, (s, t) in enumerate(zip(sources, targets))
+    sources, targets, held, sems = refs[:5], refs[5:10], refs[10:15], refs[15]
+    steps = [
+        (s.at[part], t.at[part], h.at[part])
+        for s, t, h in zip(sources, targets, held)
+        for part in (
+            [pl.ds(0, 2)] if s.shape[0] == 2 else [pl.ds(k * 256, 256) for k in range(4)]
+        )
     ]
-    for copy in copies:
+    into = [pltpu.make_async_copy(s, h, sems.at[i]) for i, (s, t, h) in enumerate(steps)]
+    out = [pltpu.make_async_copy(h, t, sems.at[i]) for i, (s, t, h) in enumerate(steps)]
+    for copy in into:
         copy.start()
-    for copy in copies:
+    for first, second in zip(into, out):
+        first.wait()
+        second.start()
+    for copy in out:
         copy.wait()
 
 
@@ -564,7 +586,7 @@
             nodes,
             nodes,
             nodes,
-            nodes,
+            pltpu.VMEM((F, NODES), BF16),
             nodes_f32,
             nodes_f32,
             nodes_f32,
@@ -619,7 +641,8 @@
         out_shape=shapes,
         in_specs=[any_space] * 5,
         out_specs=(any_space,) * 5,
-        scratch_shapes=[pltpu.SemaphoreType.DMA((5,))],
+        scratch_shapes=[pltpu.VMEM(shape.shape, shape.dtype) for shape in shapes]
+        + [pltpu.SemaphoreType.DMA((14,))],
     )(*made)
 
 

time: 244 us -> 112 us (0.46)
  Pallas kernels: 243 us -> 111 us
    pallas_call x1, Pallas kernels: 128 us -> 4.01 us  [per_device(): pl.pallas_call(deliver, out_shape=shapes, in_specs=[any_space] * 5, out_s...]
    pallas_call x1, Pallas kernels: 114 us -> 107 us  [per_device(): pl.pallas_call(kernel, out_shape=shapes, in_specs=[vmem, vmem, vmem, vmem...]
where the time goes in v4:
time: 112 us
  Pallas kernels  111 us (99%)
    pallas_call x1, Pallas kernels, per_device(): pl.pallas_call(kernel, out_shape=shapes, in_specs=[vmem, vmem, vmem, vmem...  107 us
    pallas_call x1, Pallas kernels, per_device(): pl.pallas_call(deliver, out_shape=shapes, in_specs=[any_space] * 5, out_s...  4.01 us

profile of v4, /device:TPU:1, one launch (start us, length us, event | category | flops | bytes accessed | tf_op | source)
XLA Modules:
  0.0 112.1 jit_solution(10457022048203543196)
XLA Ops:
  0.6 107.4 %shard_map.137 = (bf16[1024,512]{1,0:T(8,128)(2,1)}, bf16[1024,512]{1,0:T(8,128)(2,1)}, bf16[1024,512]{1,0:T(8,128)(2,1)}, f32[2,2,512]{2,1,0:T(2,128)}, bf16[2,512,512]{2,1,0:T(8,128)(2,1)}) custom-call(s32[8,8]{1,0:T(8,128)} %src_ref.1, s32[1,64]{1,0:T(1,128)} %sel_row_ref.1, f32[2,2,512]{2,1,0:T(2,128)} %master_ref.1, f32[2,2,512]{2,1,0:T(2,128)} %first_ref.1, ...), custom_call_target="tpu_custom_call" | custom-call | flops 12884901888 | bytes 12582912 | tf_op jit(solution)/shard_map/pallas_call | solution.py:572
  108.1 4.0 %shard_map.138 = (bf16[1024,512]{1,0:T(8,128)(2,1)}, bf16[1024,512]{1,0:T(8,128)(2,1)}, bf16[1024,512]{1,0:T(8,128)(2,1)}, f32[2,2,512]{2,1,0:T(2,128)}, bf16[2,512,512]{2,1,0:T(8,128)(2,1)}) custom-call(bf16[1024,512]{1,0:T(8,128)(2,1)} %get-tuple-element.10.refs_0_, bf16[1024,512]{1,0:T(8,128)(2,1)} %get-tuple-element.11.refs_1_, ...), custom_call_target="tpu_custom_call" | custom-call | tf_op jit(solution)/shard_map/pallas_call | solution.py:639

commit v5 on v4

--- a/solution.py
+++ b/solution.py
@@ -296,6 +296,7 @@
     spread_shard(0, shard_now, gather_now)
     loads[0].wait()
     pick_pieces(raw_send, features)
+    send_pieces(3, raw_send, rim, 1, 24)
     rim[rows_of(me, PIECE), :] = raw_send[rows_of(me, PIECE), :]
 
     tile_of = lax.broadcasted_iota(jnp.int32, (8, 1024), 1) // 128
@@ -321,20 +322,23 @@
 
     repeat(1, densify)
     gather_across(0, gather_now)
-    send_pieces(3, raw_send, rim, 1, 32)
+    send_pieces(3, raw_send, rim, 24, 64)
     repeat(3, lambda i: densify(i + 1))
     gather_core(0, gather_now)
-    send_pieces(3, raw_send, rim, 32, 64)
     repeat(4, lambda i: densify(i + 4))
 
     loads[2].wait()
     loads[4].wait()
+    loads[3].wait()
 
     def tiles_on(rows, columns, table):
         return dot(dense[rows, columns], table) + dot(dense_low[rows, columns], table)
 
     def ahead(i):
         rows = rows_of(i, 256)
+        row = lax.broadcasted_iota(jnp.int32, (256, NODES), 0) + i * 256
+        placing = (row == wanted).astype(F32).astype(BF16)
+        d_first[rows, :] = dot(placing, stale_grads[...])
         p_local[rows, :] = tiles_on(rows, slice(0, NODES), features[...])
         p_stale[rows, :] = tiles_on(rows, slice(NODES, 2 * NODES), stale_features[...])
 
@@ -362,12 +366,9 @@
     )
     own_grads.start()
 
-    loads[3].wait()
     def local_part(i):
         rows = rows_of(i, 256)
-        row = lax.broadcasted_iota(jnp.int32, (256, NODES), 0) + i * 256
-        placing = (row == wanted).astype(F32).astype(BF16)
-        d_first[rows, :] = tiles_back(rows).T + dot(placing, stale_grads[...])
+        d_first[rows, :] += tiles_back(rows).T
 
     repeat(4, local_part)
 
@@ -384,15 +385,7 @@
         dz[rows, :] = (d_first[rows, :] * s * (1.0 + zf * (1.0 - s))).astype(BF16)
 
     repeat(4, first_layer)
-    pick_pieces(feature_send, hidden)
     send_pieces(4, grad_send, fresh_grads_hbm, 48, 64)
-    own_features = pltpu.make_async_copy(
-        feature_send.at[rows_of(me, PIECE)],
-        fresh_features_hbm.at[rows_of(me, PIECE)],
-        store_sem.at[1],
-    )
-    own_features.start()
-
     def second_layer(i):
         rows = rows_of(i, 256)
         p_second[rows, :] = (p_stale[rows, :] + tiles_on(rows, slice(0, NODES), hidden[...])).astype(BF16)
@@ -429,14 +422,6 @@
     ).start()
 
 
-    def last(i):
-        rows = rows_of(i, 256)
-        layer_out[rows, :] = dot(p_second[rows, :], weights[1]).astype(BF16)
-
-    repeat(4, last)
-    store_layer = pltpu.make_async_copy(layer_out, layer_out_hbm, store_sem.at[2])
-    store_layer.start()
-
     total_of(6, from_core).wait_recv()
 
     def add_core(i):
@@ -454,7 +439,22 @@
             device_id=(z, px, c, py),
             device_id_type=MESH,
         ).start()
+    pick_pieces(feature_send, hidden)
     send_pieces(5, feature_send, fresh_features_hbm, 1, 12)
+    own_features = pltpu.make_async_copy(
+        feature_send.at[rows_of(me, PIECE)],
+        fresh_features_hbm.at[rows_of(me, PIECE)],
+        store_sem.at[1],
+    )
+    own_features.start()
+
+    def last(i):
+        rows = rows_of(i, 256)
+        layer_out[rows, :] = dot(p_second[rows, :], weights[1]).astype(BF16)
+
+    repeat(4, last)
+    store_layer = pltpu.make_async_copy(layer_out, layer_out_hbm, store_sem.at[2])
+    store_layer.start()
     total_of(7, from_across).wait_recv()
     across_total = core_sum[column].astype(F32)
     for k in range(NX * NY - 1):

time: 112 us -> 112 us (level)
  no operation moved by 1% of the time
where the time goes in v5:
time: 112 us
  Pallas kernels  111 us (99%)
    pallas_call x1, Pallas kernels, per_device(): pl.pallas_call(kernel, out_shape=shapes, in_specs=[vmem, vmem, vmem, vmem...  107 us
    pallas_call x1, Pallas kernels, per_device(): pl.pallas_call(deliver, out_shape=shapes, in_specs=[any_space] * 5, out_s...  4.01 us

profile of v5, /device:TPU:1, one launch (start us, length us, event | category | flops | bytes accessed | tf_op | source)
XLA Modules:
  0.0 111.8 jit_solution(14278288479301402210)
XLA Ops:
  0.6 107.1 %shard_map.137 = (bf16[1024,512]{1,0:T(8,128)(2,1)}, bf16[1024,512]{1,0:T(8,128)(2,1)}, bf16[1024,512]{1,0:T(8,128)(2,1)}, f32[2,2,512]{2,1,0:T(2,128)}, bf16[2,512,512]{2,1,0:T(8,128)(2,1)}) custom-call(s32[8,8]{1,0:T(8,128)} %src_ref.1, s32[1,64]{1,0:T(1,128)} %sel_row_ref.1, f32[2,2,512]{2,1,0:T(2,128)} %master_ref.1, f32[2,2,512]{2,1,0:T(2,128)} %first_ref.1, ...), custom_call_target="tpu_custom_call" | custom-call | flops 12884901888 | bytes 12582912 | tf_op jit(solution)/shard_map/pallas_call | solution.py:572
  107.8 4.0 %shard_map.138 = (bf16[1024,512]{1,0:T(8,128)(2,1)}, bf16[1024,512]{1,0:T(8,128)(2,1)}, bf16[1024,512]{1,0:T(8,128)(2,1)}, f32[2,2,512]{2,1,0:T(2,128)}, bf16[2,512,512]{2,1,0:T(8,128)(2,1)}) custom-call(bf16[1024,512]{1,0:T(8,128)(2,1)} %get-tuple-element.10.refs_0_, bf16[1024,512]{1,0:T(8,128)(2,1)} %get-tuple-element.11.refs_1_, ...), custom_call_target="tpu_custom_call" | custom-call | tf_op jit(solution)/shard_map/pallas_call | solution.py:639
